TPU v7x, 32 devices: a whole 2x2x4 slice. The times are simulated.
32 devices in a mesh: groups: 2 (over x), slab: 16 (over z, y, core).
Axes of the slice: x: 2, y: 2, z: 4, core: 2. Of those that a mesh axis runs over, the one named last changes fastest.
Arguments:
- mode_shapes: float32 [16384, 192], P(('groups', 'slab')), parts along dimension 0, may hold values from -6 to 6
- wall_coupling: float32 [16384, 15], P(('groups', 'slab')), parts along dimension 0, may hold values from -3.5 to 3.5
- owner_dev: int32 [16384, 1], P(('groups', 'slab')), parts along dimension 0, may hold values from 0 to 15; in each aligned block of 512 rows (0 to 511, 512 to 1023, ...) at most 64 rows name the same one
- owner_cell: int32 [16384], P(('groups', 'slab')), parts along dimension 0, may hold values from 0 to 2047
- neighbours: int32 [6, 65536], P(None, ('groups', 'slab')), parts along dimension 1, may hold values from -1 to 32767, as said below
- coupling_blocks: float32 [6, 5, 5, 65536], P(None, None, None, ('groups', 'slab')), parts along dimension 3, may hold values from -0.3 to 0.3
- inv_blocks: float32 [5, 5, 65536], P(None, None, ('groups', 'slab')), parts along dimension 2, may hold values from -0.9 to 3, as said below
Outputs:
- modes_basis: float32 [5, 64, 65536], P(None, None, ('groups', 'slab')), parts along dimension 2
- factor: float32 [128, 64], P('groups'), parts along dimension 0
There are 2 independent parts, one for each index of `groups`. A program takes and returns all parts, laid end to end along the dimension named above; each array names one. Nothing has to cross between parts.
Inputs may be any that keep to these rules, and one draw needn't show every extreme that they name: `owner_dev`: in the rows of one slab device at most 64 shell nodes name the same slab, a bound that some of them reach. `neighbours`: A filled slot of cell c names a cell whose number differs from c by 1 to 256. `inv_blocks`: each block has a positive diagonal entry shared by its five diagonal places and off-diagonal entries of at most 0.3 times it in magnitude.
All inputs are finite; a program needn't handle non-finite values.
Results may differ from a plain program's by a relative error of at most 0.0003.
Values sent between devices are 32-bit elements; how exact they have to be, the bound alone decides.
A program may use at most 192 MiB of HBM per device.

v0:
```python
import math

import jax
import jax.numpy as jnp
from jax import lax
from jax.sharding import PartitionSpec as P

VARS = 5
NBR = 6
SWEEPS = 2


def with_halo(x, sides, width):
    for axis, dim in sides:
        count, length = (lax.axis_size(axis), x.shape[dim])
        up = [(i, (i + 1) % count) for i in range(count - 1)]
        down = [(j, i) for i, j in up]
        last = lax.slice_in_dim(x, length - width, length, axis=dim)
        first = lax.slice_in_dim(x, 0, width, axis=dim)
        before = lax.ppermute(last, axis, up)
        after = lax.ppermute(first, axis, down)
        x = jnp.concatenate([before, x, after], axis=dim)
    return x


def apply_blocks(blocks, field_in):
    rows_out = []
    for out_var in range(field_in.shape[0]):
        summed = blocks[out_var, 0][None, :] * field_in[0]
        for in_var in range(1, field_in.shape[0]):
            summed = summed + blocks[out_var, in_var][None, :] * field_in[in_var]
        rows_out.append(summed)
    return jnp.stack(rows_out)


def couple(weights, shapes):
    node_count = weights.shape[0]
    modes_total = shapes.shape[1] // 3
    weights_split = weights.reshape(node_count, -1, 3)
    shapes_split = shapes.reshape(node_count, 3, modes_total)
    summed = weights_split[:, :, 0, None] * shapes_split[:, None, 0, :]
    for component in range(1, 3):
        summed = summed + weights_split[:, :, component, None] * shapes_split[:, None, component, :]
    return summed.reshape(node_count, -1)


def gram_matrix(left_field, right_field):
    return jnp.einsum("vpc,vqc->pq", left_field, right_field, precision=lax.Precision.HIGHEST)


def combine(coeffs, field_in):
    return jnp.einsum("pq,vpc->vqc", coeffs, field_in, precision=lax.Precision.HIGHEST)


def cholesky_upper(gram):
    order = gram.shape[0]
    places = jnp.arange(order, dtype=jnp.int32)

    def column_step(column_at, lower):
        row_now = lax.dynamic_index_in_dim(lower, column_at, 0, keepdims=False)
        target = lax.dynamic_index_in_dim(gram, column_at, 1, keepdims=False)
        reduced = target - jnp.dot(lower, row_now, precision=lax.Precision.HIGHEST)
        pivot = jnp.sqrt(lax.dynamic_index_in_dim(reduced, column_at, 0, keepdims=False))
        column = jnp.where(
            places > column_at, reduced / pivot, jnp.where(places == column_at, pivot, 0.0)
        )
        return jnp.where(places[None, :] == column_at, column[:, None], lower)

    lower = lax.fori_loop(0, order, column_step, jnp.zeros((order, order), jnp.float32))
    return lower.T


def upper_inverse(upper):
    lower = upper.T
    order = lower.shape[0]
    places = jnp.arange(order, dtype=jnp.int32)
    identity = jnp.eye(order, dtype=jnp.float32)

    def row_step(row_at, inverse):
        lower_row = lax.dynamic_index_in_dim(lower, row_at, 0, keepdims=False)
        pivot = lax.dynamic_index_in_dim(lower_row, row_at, 0, keepdims=False)
        earlier = jnp.where(places < row_at, lower_row, 0.0)
        unit_row = lax.dynamic_index_in_dim(identity, row_at, 0, keepdims=False)
        new_row = (unit_row - jnp.dot(earlier, inverse, precision=lax.Precision.HIGHEST)) / pivot
        return jnp.where(places[:, None] == row_at, new_row[None, :], inverse)

    inverse = lax.fori_loop(0, order, row_step, jnp.zeros((order, order), jnp.float32))
    return inverse.T


def local(
    mode_shapes, wall_coupling, owner_dev, owner_cell, neighbours, coupling_blocks, inv_blocks
):
    devices_slab = lax.axis_size("slab")
    cell_count = inv_blocks.shape[2]
    node_count = mode_shapes.shape[0]
    modes_total = mode_shapes.shape[1] // 3
    capacity = max(2, 2 * node_count // devices_slab)
    destination = owner_dev[:, 0]
    onehot_dest = (
        destination[:, None] == jnp.arange(devices_slab, dtype=jnp.int32)[None, :]
    ).astype(jnp.int32)
    ranking = jnp.sum((jnp.cumsum(onehot_dest, axis=0) - 1) * onehot_dest, axis=1)
    slot_of = destination * capacity + ranking
    slot_total = devices_slab * capacity
    cell_tags = (
        jnp.full((slot_total,), -1.0, jnp.float32).at[slot_of].set(owner_cell.astype(jnp.float32))
    )
    contribution = couple(wall_coupling, mode_shapes)
    outgoing = (
        jnp.zeros((slot_total, contribution.shape[1]), jnp.float32).at[slot_of].set(contribution)
    )
    arrived, arrived_tags = (
        lax.all_to_all(outgoing, "slab", split_axis=0, concat_axis=0, tiled=True),
        lax.all_to_all(cell_tags, "slab", split_axis=0, concat_axis=0, tiled=True),
    )
    matches = (
        arrived_tags.astype(jnp.int32)[:, None] == jnp.arange(cell_count, dtype=jnp.int32)[None, :]
    ).astype(jnp.float32)
    forcing = lax.dot_general(
        arrived, matches, (((0,), (0,)), ((), ())), precision=lax.Precision.HIGHEST
    )
    forcing = forcing.reshape(VARS, modes_total, cell_count)
    rim_width = cell_count // 8
    first_cell = lax.axis_index("slab") * cell_count - rim_width
    local_ids = jnp.where(neighbours >= 0, neighbours - first_cell, cell_count + 2 * rim_width)
    state_field = apply_blocks(inv_blocks, forcing)
    for sweep_step in range(SWEEPS):
        widened = with_halo(state_field, (("slab", 2),), rim_width)
        padded = jnp.concatenate(
            [widened, jnp.zeros(widened.shape[:2] + (1,), jnp.float32)], axis=2
        )
        coupled = jnp.zeros_like(state_field)
        for slot_index in range(NBR):
            gathered = jnp.take(padded, local_ids[slot_index], axis=2)
            coupled = coupled + apply_blocks(coupling_blocks[slot_index], gathered)
        state_field = apply_blocks(inv_blocks, forcing - coupled)
    block_width = modes_total // 4
    factor = jnp.zeros((modes_total, modes_total), jnp.float32)
    basis_parts = []
    for block_index in range(4):
        start_col = block_index * block_width
        panel_cols = state_field[:, start_col : start_col + block_width, :]
        if block_index > 0:
            previous = jnp.concatenate(basis_parts, axis=1)
            projection = lax.psum(gram_matrix(previous, panel_cols), "slab")
            panel_cols = panel_cols - combine(projection, previous)
            factor = factor.at[:start_col, start_col : start_col + block_width].set(projection)
        diag_block = cholesky_upper(lax.psum(gram_matrix(panel_cols, panel_cols), "slab"))
        factor = factor.at[
            start_col : start_col + block_width, start_col : start_col + block_width
        ].set(diag_block)
        basis_parts.append(combine(upper_inverse(diag_block), panel_cols))
    basis_out = jnp.concatenate(basis_parts, axis=1)
    norm_scale = math.sqrt(VARS * cell_count * devices_slab)
    return (basis_out * norm_scale, factor / norm_scale)


def solution(mesh):
    in_specs = (
        P(("groups", "slab"), None),
        P(("groups", "slab"), None),
        P(("groups", "slab"), None),
        P(("groups", "slab")),
        P(None, ("groups", "slab")),
        P(None, None, None, ("groups", "slab")),
        P(None, None, ("groups", "slab")),
    )
    out_specs = (P(None, None, ("groups", "slab")), P("groups", None))
    return jax.shard_map(local, mesh=mesh, in_specs=in_specs, out_specs=out_specs, check_vma=False)
```

profile of v0, /device:TPU:0, one launch (start us, length us, event | category | flops | bytes accessed | tf_op | source)
XLA Modules:
  0.0 1054.8 jit_solution(16598022416229044817)
XLA Ops:
  8.1 7.4 all-to-all-start.1
  52.9 27.0 %all-to-all-done = f32[16,64,320]{2,1,0:T(8,128)S(1)} async-done(((f32[16,64,320]{2,1,0:T(8,128)}), f32[16,64,320]{2,1,0:T(8,128)S(1)}, u32[]{:S(2)}, u32[]{:S(2)}) %all-to-all-start) | async-done | bytes 1310752 | tf_op jit(solution)/shard_map/all_to_all | solution.py:114
  98.3 7.6 copy.130
  105.9 19.7 %gather_fusion.5 = f32[2048,5,64]{2,1,0:T(8,128)} fusion(f32[5,64,2561]{1,0,2:T(8,128)} %copy.130, s32[2048]{0:T(1024)} %get-tuple-element.1568), kind=kCustom, calls=%fused_computation.5.clone | custom fusion | bytes 5251072 | tf_op jit(solution)/shard_map/jit(_take)/gather | solution.py:135
  131.7 19.6 %gather_fusion.4 = f32[2048,5,64]{2,1,0:T(8,128)} fusion(f32[5,64,2561]{1,0,2:T(8,128)} %copy.130, s32[2048]{0:T(1024)S(1)} %copy-done.195), kind=kCustom, calls=%fused_computation.4.clone | custom fusion | bytes 5251072 | tf_op jit(solution)/shard_map/jit(_take)/gather | solution.py:135
  157.4 19.6 %gather_fusion.3 = f32[2048,5,64]{2,1,0:T(8,128)} fusion(f32[5,64,2561]{1,0,2:T(8,128)} %copy.130, s32[2048]{0:T(1024)S(1)} %copy-done.193), kind=kCustom, calls=%fused_computation.3.clone | custom fusion | bytes 5251072 | tf_op jit(solution)/shard_map/jit(_take)/gather | solution.py:135
  183.1 19.6 %gather_fusion.2 = f32[2048,5,64]{2,1,0:T(8,128)} fusion(f32[5,64,2561]{1,0,2:T(8,128)} %copy.130, s32[2048]{0:T(1024)S(1)} %copy-done.198), kind=kCustom, calls=%fused_computation.2.clone | custom fusion | bytes 5251072 | tf_op jit(solution)/shard_map/jit(_take)/gather | solution.py:135
  208.8 19.6 %gather_fusion.1 = f32[2048,5,64]{2,1,0:T(8,128)} fusion(f32[5,64,2561]{1,0,2:T(8,128)} %copy.130, s32[2048]{0:T(1024)S(1)} %copy-done.196), kind=kCustom, calls=%fused_computation.1.clone | custom fusion | bytes 5251072 | tf_op jit(solution)/shard_map/jit(_take)/gather | solution.py:135
  234.5 19.6 %gather_fusion = f32[2048,5,64]{2,1,0:T(8,128)} fusion(f32[5,64,2561]{1,0,2:T(8,128)} %copy.130, s32[2048]{0:T(1024)S(1)} %get-tuple-element.1569), kind=kCustom, calls=%fused_computation.clone | custom fusion | bytes 5251072 | tf_op jit(solution)/shard_map/jit(_take)/gather | solution.py:135
  291.8 7.3 collective-permute-start.2
  304.6 7.6 copy.147
  312.3 19.7 %gather_fusion.11 = f32[2048,5,64]{2,1,0:T(8,128)} fusion(f32[5,64,2561]{1,0,2:T(8,128)} %copy.147, s32[2048]{0:T(1024)} %get-tuple-element.1568), kind=kCustom, calls=%fused_computation.11.clone | custom fusion | bytes 5251072 | tf_op jit(solution)/shard_map/jit(_take)/gather | solution.py:135
  332.0 19.8 %gather_fusion.10 = f32[2048,5,64]{2,1,0:T(8,128)} fusion(f32[5,64,2561]{1,0,2:T(8,128)} %copy.147, s32[2048]{0:T(1024)} %get-tuple-element.1567), kind=kCustom, calls=%fused_computation.10.clone | custom fusion | bytes 5251072 | tf_op jit(solution)/shard_map/jit(_take)/gather | solution.py:135
  351.9 19.7 %gather_fusion.9 = f32[2048,5,64]{2,1,0:T(8,128)} fusion(f32[5,64,2561]{1,0,2:T(8,128)} %copy.147, s32[2048]{0:T(1024)S(1)} %copy-done.194), kind=kCustom, calls=%fused_computation.9.clone | custom fusion | bytes 5251072 | tf_op jit(solution)/shard_map/jit(_take)/gather | solution.py:135
  371.5 19.8 %gather_fusion.8 = f32[2048,5,64]{2,1,0:T(8,128)} fusion(f32[5,64,2561]{1,0,2:T(8,128)} %copy.147, s32[2048]{0:T(1024)} %get-tuple-element.1565), kind=kCustom, calls=%fused_computation.8.clone | custom fusion | bytes 5251072 | tf_op jit(solution)/shard_map/jit(_take)/gather | solution.py:135
  391.4 19.8 %gather_fusion.7 = f32[2048,5,64]{2,1,0:T(8,128)} fusion(f32[5,64,2561]{1,0,2:T(8,128)} %copy.147, s32[2048]{0:T(1024)S(1)} %copy-done.197), kind=kCustom, calls=%fused_computation.7.clone | custom fusion | bytes 5251072 | tf_op jit(solution)/shard_map/jit(_take)/gather | solution.py:135
  411.2 19.7 %gather_fusion.6 = f32[2048,5,64]{2,1,0:T(8,128)} fusion(f32[5,64,2561]{1,0,2:T(8,128)} %copy.147, s32[2048]{0:T(1024)} %copy-done.199), kind=kCustom, calls=%fused_computation.6.clone | custom fusion | bytes 5251072 | tf_op jit(solution)/shard_map/jit(_take)/gather | solution.py:135
  511.8 37.7 %psum.49 = f32[16,16]{1,0:T(8,128)S(1)} all-reduce(f32[16,16]{1,0:T(8,128)S(1)} %convolution_bitcast_fusion.20), channel_id=1, replica_groups=mesh['groups'=2,'slab'=16] {'slab'}, use_global_device_ids=true, to_apply=%region_5.7 | all-reduce | flops 256 | bytes 2048 | tf_op jit(solution)/shard_map/psum | solution.py:149
  549.6 24.4 %while.139 = (s32[]{:T(128)}, f32[16,16]{1,0:T(8,128)S(1)}, f32[16,16]{0,1:T(8,128)S(1)}, s32[]{:T(128)}, s32[]{:T(128)}) while((s32[]{:T(128)}, f32[16,16]{1,0:T(8,128)S(1)}, f32[16,16]{0,1:T(8,128)S(1)}, s32[]{:T(128)}, s32[]{:T(128)}) %tuple.552), condition=%wide.region_7.9_spmd.clone.clone, body=%wide.region_6.8_spmd.clone.clone.sunk | while | flops 3955 | bytes 14736 | solution.py:69
  574.0 34.1 %while.140 = (s32[]{:T(128)}, f32[16,16]{1,0:T(8,128)S(1)}, f32[16,16]{1,0:T(8,128)}, f32[16,16]{1,0:T(8,128)S(1)}, s32[]{:T(128)}, /*index=5*/s32[]{:T(128)}, s32[]{:T(128)}) while((s32[]{:T(128)}, f32[16,16]{1,0:T(8,128)S(1)}, f32[16,16]{1,0:T(8,128)}, f32[16,16]{1,0:T(8,128)S(1)}, s32[]{:T(128)}, ...), condition=%wide.region_9.11_spmd.clone.clone, body=%wide.region_8.10_spmd.clone.clone.sunk | while | flops 3924 | bytes 13155 | solution.py:87
  609.8 30.0 %psum.50 = f32[16,16]{1,0:T(8,128)S(1)} all-reduce(f32[16,16]{1,0:T(8,128)S(1)} %convolution_bitcast_fusion.19), channel_id=1, replica_groups=mesh['groups'=2,'slab'=16] {'slab'}, use_global_device_ids=true, to_apply=%region_10.12 | all-reduce | flops 256 | bytes 2048 | tf_op jit(solution)/shard_map/psum | solution.py:146
  642.6 30.0 %psum.51 = f32[16,16]{1,0:T(8,128)S(1)} all-reduce(f32[16,16]{1,0:T(8,128)S(1)} %convolution_bitcast_fusion.18), channel_id=1, replica_groups=mesh['groups'=2,'slab'=16] {'slab'}, use_global_device_ids=true, to_apply=%region_11.13 | all-reduce | flops 256 | bytes 2048 | tf_op jit(solution)/shard_map/psum | solution.py:149
  672.7 24.4 %while.141 = (s32[]{:T(128)}, f32[16,16]{1,0:T(8,128)S(1)}, f32[16,16]{0,1:T(8,128)S(1)}, s32[]{:T(128)}, s32[]{:T(128)}) while((s32[]{:T(128)}, f32[16,16]{1,0:T(8,128)S(1)}, f32[16,16]{0,1:T(8,128)S(1)}, s32[]{:T(128)}, s32[]{:T(128)}) %tuple.551), condition=%wide.region_13.15_spmd.clone.clone, body=%wide.region_12.14_spmd.clone.clone.sunk | while | flops 3955 | bytes 14736 | solution.py:69
  697.1 34.1 %while.142 = (s32[]{:T(128)}, f32[16,16]{1,0:T(8,128)S(1)}, f32[16,16]{1,0:T(8,128)}, f32[16,16]{1,0:T(8,128)S(1)}, s32[]{:T(128)}, /*index=5*/s32[]{:T(128)}, s32[]{:T(128)}) while((s32[]{:T(128)}, f32[16,16]{1,0:T(8,128)S(1)}, f32[16,16]{1,0:T(8,128)}, f32[16,16]{1,0:T(8,128)S(1)}, s32[]{:T(128)}, ...), condition=%wide.region_15.17_spmd.clone.clone, body=%wide.region_14.16_spmd.clone.clone.sunk | while | flops 3924 | bytes 13155 | solution.py:87
  734.2 57.9 %psum.52 = f32[32,16]{1,0:T(8,128)S(1)} all-reduce(f32[32,16]{1,0:T(8,128)S(1)} %convolution_bitcast_fusion.15), channel_id=1, replica_groups=mesh['groups'=2,'slab'=16] {'slab'}, use_global_device_ids=true, to_apply=%region_16.18 | all-reduce | flops 512 | bytes 4096 | tf_op jit(solution)/shard_map/psum | solution.py:146
  803.9 30.0 %psum.53 = f32[16,16]{1,0:T(8,128)S(1)} all-reduce(f32[16,16]{1,0:T(8,128)S(1)} %convolution_bitcast_fusion.17), channel_id=1, replica_groups=mesh['groups'=2,'slab'=16] {'slab'}, use_global_device_ids=true, to_apply=%region_17.19 | all-reduce | flops 256 | bytes 2048 | tf_op jit(solution)/shard_map/psum | solution.py:149
  834.0 24.4 %while.143 = (s32[]{:T(128)}, f32[16,16]{1,0:T(8,128)S(1)}, f32[16,16]{0,1:T(8,128)S(1)}, s32[]{:T(128)}, s32[]{:T(128)}) while((s32[]{:T(128)}, f32[16,16]{1,0:T(8,128)S(1)}, f32[16,16]{0,1:T(8,128)S(1)}, s32[]{:T(128)}, s32[]{:T(128)}) %tuple.550), condition=%wide.region_19.21_spmd.clone.clone, body=%wide.region_18.20_spmd.clone.clone.sunk | while | flops 3955 | bytes 14736 | solution.py:69
  858.4 34.1 %while.144 = (s32[]{:T(128)}, f32[16,16]{1,0:T(8,128)S(1)}, f32[16,16]{1,0:T(8,128)}, f32[16,16]{1,0:T(8,128)S(1)}, s32[]{:T(128)}, /*index=5*/s32[]{:T(128)}, s32[]{:T(128)}) while((s32[]{:T(128)}, f32[16,16]{1,0:T(8,128)S(1)}, f32[16,16]{1,0:T(8,128)}, f32[16,16]{1,0:T(8,128)S(1)}, s32[]{:T(128)}, ...), condition=%wide.region_21.23_spmd.clone.clone, body=%wide.region_20.22_spmd.clone.clone.sunk | while | flops 3924 | bytes 13155 | solution.py:87
  896.0 57.6 %psum.54 = f32[48,16]{1,0:T(8,128)S(1)} all-reduce(f32[48,16]{1,0:T(8,128)S(1)} %fusion.90), channel_id=1, replica_groups=mesh['groups'=2,'slab'=16] {'slab'}, use_global_device_ids=true, to_apply=%region_22.24 | all-reduce | flops 768 | bytes 6144 | tf_op jit(solution)/shard_map/psum | solution.py:146
  962.0 30.0 %psum.55 = f32[16,16]{1,0:T(8,128)S(1)} all-reduce(f32[16,16]{1,0:T(8,128)S(1)} %convolution_bitcast_fusion.16), channel_id=1, replica_groups=mesh['groups'=2,'slab'=16] {'slab'}, use_global_device_ids=true, to_apply=%region_23.25 | all-reduce | flops 256 | bytes 2048 | tf_op jit(solution)/shard_map/psum | solution.py:149
  992.1 24.4 %while.145 = (s32[]{:T(128)}, f32[16,16]{1,0:T(8,128)S(1)}, f32[16,16]{0,1:T(8,128)S(1)}, s32[]{:T(128)}, s32[]{:T(128)}) while((s32[]{:T(128)}, f32[16,16]{1,0:T(8,128)S(1)}, f32[16,16]{0,1:T(8,128)S(1)}, s32[]{:T(128)}, s32[]{:T(128)}) %tuple.549), condition=%wide.region_25.27_spmd.clone.clone, body=%wide.region_24.26_spmd.clone.clone.sunk | while | flops 3955 | bytes 14736 | solution.py:69
  1016.6 34.1 %while.146 = (s32[]{:T(128)}, f32[16,16]{1,0:T(8,128)S(1)}, f32[16,16]{1,0:T(8,128)}, f32[16,16]{1,0:T(8,128)S(1)}, s32[]{:T(128)}, /*index=5*/s32[]{:T(128)}, s32[]{:T(128)}) while((s32[]{:T(128)}, f32[16,16]{1,0:T(8,128)S(1)}, f32[16,16]{1,0:T(8,128)}, f32[16,16]{1,0:T(8,128)S(1)}, s32[]{:T(128)}, ...), condition=%wide.region_27.29_spmd.clone.clone, body=%wide.region_26.28_spmd.clone.clone.sunk | while | flops 3924 | bytes 13155 | solution.py:87
  (1295 shorter events, 438.7 us)
Async XLA Ops:
  8.1 33.1 %all-to-all-start.1 = ((f32[16,64,1]{1,2,0:T(1,128)}), f32[16,64,1]{1,2,0:T(1,128)S(1)}, u32[]{:S(2)}, u32[]{:S(2)}) async-start(f32[16,64,1]{1,2,0:T(1,128)} %bitcast.16), calls=%async_computation.1 | async-start | bytes 16384 | tf_op jit(solution)/shard_map/all_to_all | solution.py:115
  41.8 38.2 %all-to-all-start = ((f32[16,64,320]{2,1,0:T(8,128)}), f32[16,64,320]{2,1,0:T(8,128)S(1)}, u32[]{:S(2)}, u32[]{:S(2)}) async-start(f32[16,64,320]{2,1,0:T(8,128)} %bitcast.14), calls=%async_computation | async-start | bytes 3145728 | tf_op jit(solution)/shard_map/all_to_all | solution.py:114
  51.6 223.7 %copy-start.129 = (f32[1,1,2048]{2,1,0:T(1,128)}, f32[1,1,2048]{2,1,0:T(1,128)S(1)}, u32[]{:S(2)}) copy-start(f32[1,1,2048]{2,1,0:T(1,128)S(1)} %get-tuple-element.1472) | copy-start | bytes 24580
  51.8 224.3 %copy-start.121 = (f32[1,1,2048]{2,1,0:T(1,128)}, f32[1,1,2048]{2,1,0:T(1,128)S(1)}, u32[]{:S(2)}) copy-start(f32[1,1,2048]{2,1,0:T(1,128)S(1)} %get-tuple-element.1462) | copy-start | bytes 24580
  51.8 224.3 %copy-start.123 = (f32[1,1,2048]{2,1,0:T(1,128)}, f32[1,1,2048]{2,1,0:T(1,128)S(1)}, u32[]{:S(2)}) copy-start(f32[1,1,2048]{2,1,0:T(1,128)S(1)} %get-tuple-element.1463) | copy-start | bytes 24580
  51.8 224.3 %copy-start.125 = (f32[1,1,2048]{2,1,0:T(1,128)}, f32[1,1,2048]{2,1,0:T(1,128)S(1)}, u32[]{:S(2)}) copy-start(f32[1,1,2048]{2,1,0:T(1,128)S(1)} %get-tuple-element.1464) | copy-start | bytes 24580
  51.8 224.3 %copy-start.127 = (f32[1,1,2048]{2,1,0:T(1,128)}, f32[1,1,2048]{2,1,0:T(1,128)S(1)}, u32[]{:S(2)}) copy-start(f32[1,1,2048]{2,1,0:T(1,128)S(1)} %get-tuple-element.1465) | copy-start | bytes 24580
  51.8 224.5 %copy-start.111 = (f32[1,1,2048]{2,1,0:T(1,128)}, f32[1,1,2048]{2,1,0:T(1,128)S(1)}, u32[]{:S(2)}) copy-start(f32[1,1,2048]{2,1,0:T(1,128)S(1)} %get-tuple-element.1457) | copy-start | bytes 24580
  51.8 224.5 %copy-start.113 = (f32[1,1,2048]{2,1,0:T(1,128)}, f32[1,1,2048]{2,1,0:T(1,128)S(1)}, u32[]{:S(2)}) copy-start(f32[1,1,2048]{2,1,0:T(1,128)S(1)} %get-tuple-element.1458) | copy-start | bytes 24580
  51.8 224.5 %copy-start.115 = (f32[1,1,2048]{2,1,0:T(1,128)}, f32[1,1,2048]{2,1,0:T(1,128)S(1)}, u32[]{:S(2)}) copy-start(f32[1,1,2048]{2,1,0:T(1,128)S(1)} %get-tuple-element.1459) | copy-start | bytes 24580
  51.8 224.5 %copy-start.117 = (f32[1,1,2048]{2,1,0:T(1,128)}, f32[1,1,2048]{2,1,0:T(1,128)S(1)}, u32[]{:S(2)}) copy-start(f32[1,1,2048]{2,1,0:T(1,128)S(1)} %get-tuple-element.1460) | copy-start | bytes 24580
  51.8 224.5 %copy-start.119 = (f32[1,1,2048]{2,1,0:T(1,128)}, f32[1,1,2048]{2,1,0:T(1,128)S(1)}, u32[]{:S(2)}) copy-start(f32[1,1,2048]{2,1,0:T(1,128)S(1)} %get-tuple-element.1461) | copy-start | bytes 24580
  51.9 224.7 %copy-start.101 = (f32[1,1,2048]{2,1,0:T(1,128)}, f32[1,1,2048]{2,1,0:T(1,128)S(1)}, u32[]{:S(2)}) copy-start(f32[1,1,2048]{2,1,0:T(1,128)S(1)} %get-tuple-element.1452) | copy-start | bytes 24580
  51.9 224.7 %copy-start.103 = (f32[1,1,2048]{2,1,0:T(1,128)}, f32[1,1,2048]{2,1,0:T(1,128)S(1)}, u32[]{:S(2)}) copy-start(f32[1,1,2048]{2,1,0:T(1,128)S(1)} %get-tuple-element.1453) | copy-start | bytes 24580
  51.9 224.7 %copy-start.105 = (f32[1,1,2048]{2,1,0:T(1,128)}, f32[1,1,2048]{2,1,0:T(1,128)S(1)}, u32[]{:S(2)}) copy-start(f32[1,1,2048]{2,1,0:T(1,128)S(1)} %get-tuple-element.1454) | copy-start | bytes 24580
  51.9 224.7 %copy-start.107 = (f32[1,1,2048]{2,1,0:T(1,128)}, f32[1,1,2048]{2,1,0:T(1,128)S(1)}, u32[]{:S(2)}) copy-start(f32[1,1,2048]{2,1,0:T(1,128)S(1)} %get-tuple-element.1455) | copy-start | bytes 24580
  51.9 224.7 %copy-start.109 = (f32[1,1,2048]{2,1,0:T(1,128)}, f32[1,1,2048]{2,1,0:T(1,128)S(1)}, u32[]{:S(2)}) copy-start(f32[1,1,2048]{2,1,0:T(1,128)S(1)} %get-tuple-element.1456) | copy-start | bytes 24580
  51.9 225.0 %copy-start.91 = (f32[1,1,2048]{2,1,0:T(1,128)}, f32[1,1,2048]{2,1,0:T(1,128)S(1)}, u32[]{:S(2)}) copy-start(f32[1,1,2048]{2,1,0:T(1,128)S(1)} %get-tuple-element.1447) | copy-start | bytes 24580
  51.9 225.0 %copy-start.93 = (f32[1,1,2048]{2,1,0:T(1,128)}, f32[1,1,2048]{2,1,0:T(1,128)S(1)}, u32[]{:S(2)}) copy-start(f32[1,1,2048]{2,1,0:T(1,128)S(1)} %get-tuple-element.1448) | copy-start | bytes 24580
  51.9 225.0 %copy-start.95 = (f32[1,1,2048]{2,1,0:T(1,128)}, f32[1,1,2048]{2,1,0:T(1,128)S(1)}, u32[]{:S(2)}) copy-start(f32[1,1,2048]{2,1,0:T(1,128)S(1)} %get-tuple-element.1449) | copy-start | bytes 24580
  51.9 225.0 %copy-start.97 = (f32[1,1,2048]{2,1,0:T(1,128)}, f32[1,1,2048]{2,1,0:T(1,128)S(1)}, u32[]{:S(2)}) copy-start(f32[1,1,2048]{2,1,0:T(1,128)S(1)} %get-tuple-element.1450) | copy-start | bytes 24580
  51.9 225.0 %copy-start.99 = (f32[1,1,2048]{2,1,0:T(1,128)}, f32[1,1,2048]{2,1,0:T(1,128)S(1)}, u32[]{:S(2)}) copy-start(f32[1,1,2048]{2,1,0:T(1,128)S(1)} %get-tuple-element.1451) | copy-start | bytes 24580
  52.1 225.5 %copy-start.83 = (f32[1,1,2048]{2,1,0:T(1,128)}, f32[1,1,2048]{2,1,0:T(1,128)S(1)}, u32[]{:S(2)}) copy-start(f32[1,1,2048]{2,1,0:T(1,128)S(1)} %get-tuple-element.1437) | copy-start | bytes 24580
  52.1 225.5 %copy-start.85 = (f32[1,1,2048]{2,1,0:T(1,128)}, f32[1,1,2048]{2,1,0:T(1,128)S(1)}, u32[]{:S(2)}) copy-start(f32[1,1,2048]{2,1,0:T(1,128)S(1)} %get-tuple-element.1438) | copy-start | bytes 24580
  52.1 225.5 %copy-start.87 = (f32[1,1,2048]{2,1,0:T(1,128)}, f32[1,1,2048]{2,1,0:T(1,128)S(1)}, u32[]{:S(2)}) copy-start(f32[1,1,2048]{2,1,0:T(1,128)S(1)} %get-tuple-element.1439) | copy-start | bytes 24580
  52.1 225.5 %copy-start.89 = (f32[1,1,2048]{2,1,0:T(1,128)}, f32[1,1,2048]{2,1,0:T(1,128)S(1)}, u32[]{:S(2)}) copy-start(f32[1,1,2048]{2,1,0:T(1,128)S(1)} %get-tuple-element.1440) | copy-start | bytes 24580
  52.1 225.8 %copy-start.79 = (f32[1,1,2048]{2,1,0:T(1,128)}, f32[1,1,2048]{2,1,0:T(1,128)S(1)}, u32[]{:S(2)}) copy-start(f32[1,1,2048]{2,1,0:T(1,128)S(1)} %get-tuple-element.1435) | copy-start | bytes 24580
  52.1 225.8 %copy-start.81 = (f32[1,1,2048]{2,1,0:T(1,128)}, f32[1,1,2048]{2,1,0:T(1,128)S(1)}, u32[]{:S(2)}) copy-start(f32[1,1,2048]{2,1,0:T(1,128)S(1)} %get-tuple-element.1436) | copy-start | bytes 24580
  88.5 5.1 collective-permute-start
  91.2 5.0 collective-permute-start.1
  291.8 10.5 collective-permute-start.2
  299.1 3.5 collective-permute-start.3
  (193 other events, 4023.8 us)
where the time goes:
time: 1070 us; the launch traced here: 1050 us
  local copies, waits for them, and re-layouts  451 us (42%)
  blocking collectives  273 us (26%)
  matrix products  127 us (12%)
  other arithmetic  98.8 us (9%)
  loops' own time  45.6 us (4%)
  waiting for transfers between devices  30 us (3%)
  starting transfers between devices  26.2 us (2%)
    gather x24, local copies, waits for them, and re-layouts, local(): gathered = jnp.take(padded, local_ids[slot_index], axis=2)  310 us
    psum x3, blocking collectives, local(): projection = lax.psum(gram_matrix(previous, panel_cols), 'slab')  146 us
    psum x4, blocking collectives, local(): lax.psum(gram_matrix(panel_cols, panel_cols), 'slab')  128 us
    dot_general x64, matrix products, row_step(): jnp.dot(earlier, inverse, precision=lax.Precision.HIGHEST)  93.2 us
    another operation x4, loops' own time, cholesky_upper(): lax.fori_loop(0, order, column_step, jnp.zeros((order, order), jnp.float32))  45.1 us
    dynamic_slice x64, local copies, waits for them, and re-layouts, column_step(): lax.dynamic_index_in_dim(reduced, column_at, 0, keepdims=False)  38 us
    dynamic_slice x64, local copies, waits for them, and re-layouts, row_step(): pivot = lax.dynamic_index_in_dim(lower_row, row_at, 0, keepdims=False)  37.7 us
    unnamed x68, other arithmetic  29.4 us
  transfers between devices with their start and end apart: 6, of which 3 were waited for; matrix products, arithmetic and copies ran while one was open for 3% of the time, Pallas kernels for 0%

commit v1 on v0

v1 whole, which is shorter than its diff:
```python
import functools
import math

import jax
import jax.numpy as jnp
from jax import lax
from jax.experimental import pallas as pl
from jax.experimental.pallas import tpu as pltpu
from jax.sharding import PartitionSpec as P

VARS = 5
NBR = 6
COMPS = 3
LANES = 128
TILES = 8
MESH = pl.DeviceIdType.MESH
F32 = jnp.float32
BF16 = jnp.bfloat16


def split_two(value):
    high = value.astype(BF16)
    low = (value - high.astype(F32)).astype(BF16)
    return high, low


def dot_f32(left, right):
    return jnp.dot(left, right, preferred_element_type=F32)


def kernel(
    count, cap, modes, cells, scale,
    payload_ref, dest_ref, nbr_ref, coupling_ref, inv_ref,
    basis_ref, factor_ref,
    outgoing, arrived, loads, tag_rows, hot, scaled, start, first, second, gathered,
    edges, halos, part, sums, whole,
    send_a, recv_a, send_h, recv_h, send_g, recv_g, send_w, recv_w,
):
    me = lax.axis_index("slab")
    nodes = dest_ref.shape[0]
    groups = LANES // cap
    width = modes // groups
    rows = COMPS * width + 16
    tall = VARS * modes
    span = cells // TILES
    step = count // TILES

    def remote(src, dst, send, recv, peer):
        return pltpu.make_async_remote_copy(
            src_ref=src, dst_ref=dst, send_sem=send, recv_sem=recv,
            device_id={"slab": peer}, device_id_type=MESH,
        )

    barrier = pltpu.get_barrier_semaphore()
    for shift in range(1, count):
        pl.semaphore_signal(
            barrier, inc=1, device_id={"slab": lax.rem(me + shift, count)}, device_id_type=MESH
        )
    halos[...] = jnp.zeros_like(halos)

    dest = dest_ref[...]
    lane = lax.broadcasted_iota(jnp.int32, (nodes, LANES), 1)
    names = dest == lane
    earlier = (
        lax.broadcasted_iota(jnp.int32, (nodes, nodes), 1)
        < lax.broadcasted_iota(jnp.int32, (nodes, nodes), 0)
    )
    before = dot_f32(earlier.astype(F32).astype(BF16), names.astype(F32).astype(BF16))
    rank = jnp.sum(jnp.where(names, before, 0.0), axis=1, keepdims=True).astype(jnp.int32)
    place = dest * LANES + rank
    turned = payload_ref[...].T
    pieces = []
    for group in range(groups):
        taken = [
            turned[comp * modes + group * width : comp * modes + (group + 1) * width]
            for comp in range(COMPS)
        ]
        pieces.append(jnp.concatenate(taken + [turned[COMPS * modes : COMPS * modes + 16]], axis=0))
    packed = jnp.concatenate(split_two(jnp.concatenate(pieces, axis=1)), axis=0)

    def pack_for(slab):
        at = place - slab * LANES
        picks = jnp.concatenate(
            [(at + group * cap == lane).astype(F32).astype(BF16) for group in range(groups)], axis=0
        )
        both = dot_f32(packed, picks)
        return both[:rows] + both[rows:]

    pl.semaphore_wait(barrier, count - 1)

    def send_step(shift, carry):
        slab = lax.rem(me + shift, count)
        outgoing[slab] = pack_for(slab)
        remote(outgoing.at[slab], arrived.at[me], send_a.at[slab], recv_a.at[me], slab).start()
        return carry

    lax.fori_loop(1, count, send_step, 0)
    arrived[me] = pack_for(me)

    first_cell = me * cells - span
    window = lax.broadcasted_iota(jnp.int32, (3 * span, span), 0)

    def hot_step(block, carry):
        at = pl.ds(pl.multiple_of(block * span, span), span)
        for slot in range(NBR):
            names_now = nbr_ref[slot : slot + 1, at]
            local = jnp.where(names_now >= 0, names_now - (first_cell + block * span), -1)
            hot[block, :, slot * span : (slot + 1) * span] = (window == local).astype(F32).astype(BF16)
        return carry

    lax.fori_loop(0, TILES, hot_step, 0)

    def scale_step(slot, carry):
        for out_var in range(VARS):
            total = inv_ref[out_var, 0:1, :] * coupling_ref[slot, 0]
            for mid in range(1, VARS):
                total = total + inv_ref[out_var, mid : mid + 1, :] * coupling_ref[slot, mid]
            scaled[slot, out_var] = total
        return carry

    lax.fori_loop(0, NBR, scale_step, 0)

    def arrive_step(shift, carry):
        slab = lax.rem(me + shift, count)
        remote(outgoing.at[slab], arrived.at[slab], send_a.at[slab], recv_a.at[slab], slab).wait()
        return carry

    lax.fori_loop(1, count, arrive_step, 0)

    part_of = lax.broadcasted_iota(jnp.int32, (1, LANES), 1) // cap

    def load_step(bunch, carry):
        at = pl.ds(pl.multiple_of(bunch * LANES, LANES), LANES)
        tags = jnp.zeros((1, LANES), F32)
        built = [[None] * groups for _ in range(VARS)]
        for turn in range(groups):
            here = part_of == turn
            data = arrived[bunch * groups + turn]
            base = COMPS * width
            tags = jnp.where(here, data[base + 15 : base + 16], tags)
            for var in range(VARS):
                load = data[base + COMPS * var : base + COMPS * var + 1] * data[:width]
                for comp in range(1, COMPS):
                    at_row = base + COMPS * var + comp
                    load = load + data[at_row : at_row + 1] * data[comp * width : (comp + 1) * width]
                for group in range(groups):
                    turn_by = ((turn - group) * cap) % LANES
                    moved = pltpu.roll(load, turn_by, 1) if turn_by else load
                    kept = built[var][group]
                    built[var][group] = moved if kept is None else jnp.where(here, moved, kept)
        for var in range(VARS):
            high, low = split_two(jnp.concatenate(built[var], axis=0))
            loads[var * modes : (var + 1) * modes, at] = high
            loads[tall + var * modes : tall + (var + 1) * modes, at] = low
        tag_rows[:, at] = jnp.broadcast_to(tags, (8, LANES))
        return carry

    lax.fori_loop(0, count // groups, load_step, 0)
    tag_column = tag_rows[...].T[:, 0:1].astype(jnp.int32)
    slot_cells = lax.broadcasted_iota(jnp.int32, (count * cap, span), 1)

    def keep(state, block, var, value):
        high, low = split_two(value)
        state[block + 1, var * modes : (var + 1) * modes] = high
        state[block + 1, tall + var * modes : tall + (var + 1) * modes] = low

    def begin(block, side):
        at = pl.ds(pl.multiple_of(block * span, span), span)
        matches = (tag_column == slot_cells + block * span).astype(F32).astype(BF16)
        both = dot_f32(loads[...], matches)
        forcing = both[:tall] + both[tall:]
        for var in range(VARS):
            total = inv_ref[var, 0:1, at] * forcing[:modes]
            for mid in range(1, VARS):
                total = total + inv_ref[var, mid : mid + 1, at] * forcing[mid * modes : (mid + 1) * modes]
            start[block, var * modes : (var + 1) * modes] = total
            keep(first, block, var, total)
            if side is not None:
                edges[0, side, var * modes : (var + 1) * modes] = total

    def sweep(source, target, block, side):
        at = pl.ds(pl.multiple_of(block * span, span), span)
        near = jnp.concatenate([source[block], source[block + 1], source[block + 2]], axis=1)
        for slot in range(NBR):
            both = dot_f32(near, hot[block, :, slot * span : (slot + 1) * span])
            gathered[slot] = both[:tall] + both[tall:]
        for var in range(VARS):
            total = start[block, var * modes : (var + 1) * modes]
            for slot in range(NBR):
                for mid in range(VARS):
                    total = total - (
                        scaled[slot, var, mid : mid + 1, at]
                        * gathered[slot, mid * modes : (mid + 1) * modes]
                    )
            keep(target, block, var, total)
            if side is not None:
                edges[1, side, var * modes : (var + 1) * modes] = total

    def halo_copy(turn, side):
        peer = me - 1 if side == 0 else me + 1
        return remote(
            edges.at[turn, side], halos.at[turn, 1 - side],
            send_h.at[turn, side], recv_h.at[turn, 1 - side], peer,
        )

    def halo_wait(turn, side):
        peer = me - 1 if side == 0 else me + 1
        return remote(
            edges.at[turn, side], halos.at[turn, side],
            send_h.at[turn, side], recv_h.at[turn, side], peer,
        )

    def halo_send(turn):
        @pl.when(me > 0)
        def _():
            halo_copy(turn, 0).start()

        @pl.when(me < count - 1)
        def _():
            halo_copy(turn, 1).start()

    def halo_take(turn, state):
        @pl.when(me > 0)
        def _():
            halo_wait(turn, 0).wait()

        @pl.when(me < count - 1)
        def _():
            halo_wait(turn, 1).wait()

        for side, block in ((0, -1), (1, TILES)):
            for var in range(VARS):
                keep(state, block, var, halos[turn, side, var * modes : (var + 1) * modes])

    last = TILES - 1
    begin(0, 0)
    begin(last, 1)
    halo_send(0)

    def begin_step(block, carry):
        begin(block, None)
        return carry

    lax.fori_loop(1, last, begin_step, 0)

    def first_step(block, carry):
        sweep(first, second, block, None)
        return carry

    def second_step(block, carry):
        sweep(second, first, block, None)
        return carry

    lax.fori_loop(1, TILES // 2, first_step, 0)
    halo_take(0, first)
    sweep(first, second, 0, 0)
    sweep(first, second, last, 1)
    halo_send(1)
    lax.fori_loop(TILES // 2, last, first_step, 0)
    lax.fori_loop(1, last, second_step, 0)
    halo_take(1, second)
    sweep(second, first, 0, None)
    sweep(second, first, last, None)

    def gram_step(block, total):
        for var in range(VARS):
            stack = jnp.concatenate(
                [
                    first[block + 1, var * modes : (var + 1) * modes],
                    first[block + 1, tall + var * modes : tall + (var + 1) * modes],
                ],
                axis=0,
            )
            total = total + lax.dot_general(
                stack, stack, (((1,), (1,)), ((), ())), preferred_element_type=F32
            )
        return total

    gram = lax.fori_loop(0, TILES, gram_step, jnp.zeros((2 * modes, 2 * modes), F32))
    gram = gram[:modes] + gram[modes:]
    gram = gram + pltpu.roll(gram, modes, 1)
    high = modes // TILES
    for tile in range(TILES):
        owner = tile * step
        part[tile] = gram[tile * high : (tile + 1) * high]

        @pl.when(me != owner)
        def _():
            remote(part.at[tile], sums.at[me], send_g.at[tile], recv_g.at[me], owner).start()

        @pl.when(me == owner)
        def _():
            sums[me] = part[tile]

    mine = me // step

    @pl.when(lax.rem(me, step) == 0)
    def _():
        def sum_wait(shift, carry):
            slab = lax.rem(me + shift, count)
            remote(part.at[0], sums.at[slab], send_g.at[0], recv_g.at[slab], slab).wait_recv()
            return carry

        lax.fori_loop(1, count, sum_wait, 0)
        total = sums[0]
        for slab in range(1, count):
            total = total + sums[slab]
        whole[mine] = total
        for shift in range(1, count):
            slab = lax.rem(me + shift, count)
            remote(whole.at[mine], whole.at[mine], send_w.at[slab], recv_w.at[mine], slab).start()

    for tile in range(TILES):
        owner = tile * step

        @pl.when(me != owner)
        def _():
            remote(part.at[tile], sums.at[me], send_g.at[tile], recv_g.at[me], owner).wait_send()
            remote(whole.at[tile], whole.at[tile], send_w.at[0], recv_w.at[tile], owner).wait_recv()

    row_at = lax.broadcasted_iota(jnp.int32, (modes, 2 * modes), 0)
    col_at = lax.broadcasted_iota(jnp.int32, (modes, 2 * modes), 1)
    table = jnp.concatenate([whole[tile] for tile in range(TILES)], axis=0)
    table = jnp.where(col_at < modes, table, jnp.where(col_at - modes == row_at, 1.0, 0.0))
    bands = [table[tile * high : (tile + 1) * high] for tile in range(TILES)]
    inner = lax.broadcasted_iota(jnp.int32, (high, 1), 0)
    for pivot_at in range(modes):
        band, offset = pivot_at // high, pivot_at % high
        row = bands[band][offset : offset + 1]
        row = row * (1.0 / row[:, pivot_at : pivot_at + 1])
        for tile in range(band, TILES):
            column = bands[tile][:, pivot_at : pivot_at + 1]
            if tile == band:
                column = jnp.where(inner > offset, column, 0.0)
            bands[tile] = bands[tile] - column * row
    table = jnp.concatenate(bands, axis=0)
    diagonal = jnp.sum(jnp.where(col_at == row_at, table, 0.0), axis=1, keepdims=True)
    root = jnp.sqrt(diagonal)
    factor_ref[...] = jnp.where(col_at >= row_at, table * (root / diagonal) * (1.0 / scale), 0.0)[:, :modes]
    inverse = pltpu.roll(table * (scale / root), modes, 1)[:, :modes]
    inv_high, inv_low = split_two(inverse)
    mixer = jnp.concatenate([inv_high, inv_high, inv_low], axis=1)

    def basis_step(block, carry):
        at = pl.ds(pl.multiple_of(block * span, span), span)
        for var in range(VARS):
            top = first[block + 1, var * modes : (var + 1) * modes]
            bottom = first[block + 1, tall + var * modes : tall + (var + 1) * modes]
            basis_ref[var, :, at] = dot_f32(mixer, jnp.concatenate([top, bottom, top], axis=0))
        return carry

    lax.fori_loop(0, TILES, basis_step, 0)

    @pl.when(lax.rem(me, step) == 0)
    def _():
        for shift in range(1, count):
            slab = lax.rem(me + shift, count)
            remote(whole.at[mine], whole.at[mine], send_w.at[slab], recv_w.at[mine], slab).wait_send()


def local(
    mode_shapes, wall_coupling, owner_dev, owner_cell, neighbours, coupling_blocks, inv_blocks
):
    count = lax.axis_size("slab")
    cells = inv_blocks.shape[2]
    nodes = mode_shapes.shape[0]
    modes = mode_shapes.shape[1] // COMPS
    cap = max(2, 2 * nodes // count)
    groups = LANES // cap
    rows = COMPS * (modes // groups) + 16
    tall = VARS * modes
    span = cells // TILES
    payload = jnp.concatenate(
        [mode_shapes, wall_coupling, owner_cell.astype(F32)[:, None], jnp.zeros((nodes, 48), F32)], axis=1
    )
    scale = math.sqrt(VARS * cells * count)
    vmem = pl.BlockSpec(memory_space=pltpu.VMEM)
    dma = pltpu.SemaphoreType.DMA
    return pl.pallas_call(
        functools.partial(kernel, count, cap, modes, cells, scale),
        out_shape=(
            jax.ShapeDtypeStruct((VARS, modes, cells), F32),
            jax.ShapeDtypeStruct((modes, modes), F32),
        ),
        in_specs=[vmem] * 5,
        out_specs=(vmem, vmem),
        scratch_shapes=[
            pltpu.VMEM((count, rows, LANES), F32),
            pltpu.VMEM((count, rows, LANES), F32),
            pltpu.VMEM((2 * tall, count * cap), BF16),
            pltpu.VMEM((8, count * cap), F32),
            pltpu.VMEM((TILES, 3 * span, NBR * span), BF16),
            pltpu.VMEM((NBR, VARS, VARS, cells), F32),
            pltpu.VMEM((TILES, tall, span), F32),
            pltpu.VMEM((TILES + 2, 2 * tall, span), BF16),
            pltpu.VMEM((TILES + 2, 2 * tall, span), BF16),
            pltpu.VMEM((NBR, tall, span), F32),
            pltpu.VMEM((2, 2, tall, span), F32),
            pltpu.VMEM((2, 2, tall, span), F32),
            pltpu.VMEM((TILES, modes // TILES, 2 * modes), F32),
            pltpu.VMEM((count, modes // TILES, 2 * modes), F32),
            pltpu.VMEM((TILES, modes // TILES, 2 * modes), F32),
            dma((count,)), dma((count,)), dma((2, 2)), dma((2, 2)),
            dma((TILES,)), dma((count,)), dma((count,)), dma((TILES,)),
        ],
        compiler_params=pltpu.CompilerParams(
            collective_id=0, has_side_effects=True, vmem_limit_bytes=58 * 1024 * 1024
        ),
    )(payload, owner_dev, neighbours, coupling_blocks, inv_blocks)


def solution(mesh):
    in_specs = (
        P(("groups", "slab"), None),
        P(("groups", "slab"), None),
        P(("groups", "slab"), None),
        P(("groups", "slab")),
        P(None, ("groups", "slab")),
        P(None, None, None, ("groups", "slab")),
        P(None, None, ("groups", "slab")),
    )
    out_specs = (P(None, None, ("groups", "slab")), P("groups", None))
    return jax.shard_map(local, mesh=mesh, in_specs=in_specs, out_specs=out_specs, check_vma=False)
```

time: 1070 us -> 106 us (0.10); the launches traced: 1050 us -> 106 us
  local copies, waits for them, and re-layouts: 451 us -> 10 us
  blocking collectives: 273 us -> 0 us
  matrix products: 127 us -> 0 us
  other arithmetic: 98.8 us -> 1.8 us
  Pallas kernels: 0 us -> 93.1 us
  loops' own time: 45.6 us -> 0 us
  waiting for transfers between devices: 30 us -> 0 us
  starting transfers between devices: 26.2 us -> 0 us
    gather x24 -> x0, local copies, waits for them, and re-layouts: 310 us -> none  [local(): gathered = jnp.take(padded, local_ids[slot_index], axis=2)]
    psum x7 -> x0, blocking collectives: 273 us -> none  [the longest x3 146 us: local(): projection = lax.psum(gram_matrix(previous, panel_cols), 'slab')]
    dot_general x143 -> x0, matrix products: 127 us -> none  [the longest x64 93.2 us: row_step(): jnp.dot(earlier, inverse, precision=lax.Precision.HIGHEST)]
    pallas_call x0 -> x1, Pallas kernels: none -> 93.1 us  [local(): pl.pallas_call(functools.partial(kernel, count, cap, modes, cells, scale)...]
    dynamic_slice x128 -> x0, local copies, waits for them, and re-layouts: 75.7 us -> none  [the longest x64 38 us: column_step(): lax.dynamic_index_in_dim(reduced, column_at, 0, keepdims=False)]
    another operation x8 -> x0, loops' own time: 45.6 us -> none  [the longest x4 45.1 us: cholesky_upper(): lax.fori_loop(0, order, column_step, jnp.zeros((order, order), jnp.float32))]
    unnamed x68 -> x0, other arithmetic: 29.4 us -> none
    all_to_all x2 -> x0, waiting for transfers between devices: 27 us -> none  [the longest x1 27 us: local(): lax.all_to_all(outgoing, 'slab', split_axis=0, concat_axis=0, tiled=True)]
  transfers between devices with their start and end apart: 6 -> 0, of which waited for: 3 -> 0; matrix products, arithmetic and copies ran while one was open for 3% -> 0% of each run, Pallas kernels for 0% -> 0%
where the time goes in v1:
time: 106 us
  Pallas kernels  93.1 us (88%)
  local copies, waits for them, and re-layouts  10 us (9%)
  other arithmetic  1.8 us (2%)
    pallas_call x1, Pallas kernels, local(): pl.pallas_call(functools.partial(kernel, count, cap, modes, cells, scale)...  93.1 us
    unnamed x10, local copies, waits for them, and re-layouts  9.81 us

profile of v1, /device:TPU:0, one launch (start us, length us, event | category | flops | bytes accessed | tf_op | source)
XLA Modules:
  0.0 105.6 jit_solution(1419156905758078394)
XLA Ops:
  0.6 0.0 copy-start
  0.6 0.1 pad.3.clone
  0.7 0.8 convert_element_type.3
  1.5 0.1 copy.15
  1.7 0.9 copy.14
  2.6 1.5 %copy.16.dest_ref = s32[512,1]{1,0:T(8,128)} copy(s32[512,1]{0,1:T(1,128)} %param.9) | data formatting | bytes 4096 | tf_op args[2]
  4.1 1.2 %copy.13 = f32[512,192]{1,0:T(8,128)S(1)} copy(f32[512,192]{0,1:T(8,128)} %param.7) | data formatting | bytes 786432 | tf_op args[0]
  5.3 1.0 maximum_maximum_fusion.payload_ref
  6.3 0.0 copy-done
  6.3 2.0 %copy.17.coupling_ref = f32[6,5,5,2048]{3,2,1,0:T(8,128)} copy(f32[6,5,5,2048]{3,0,2,1:T(8,128)S(1)} %copy-done) | data formatting | bytes 2457600 | tf_op args[5]
  8.3 93.1 %shard_map.86 = (f32[5,64,2048]{2,1,0:T(8,128)}, f32[64,64]{1,0:T(8,128)}) custom-call(f32[512,256]{1,0:T(8,128)} %maximum_maximum_fusion.payload_ref, s32[512,1]{1,0:T(8,128)} %copy.16.dest_ref, s32[6,2048]{1,0:T(8,128)} %nbr_ref.1, f32[6,5,5,2048]{3,2,1,0:T(8,128)} %copy.17.coupling_ref, f32[5,5,2048]{2,1,0:T(8,128)} %inv_ref.1), custom_call_target="tpu_custom_call" | custom-call | tf_op jit(solution)/shard_map/pallas_call | solution.py:379
  101.4 0.0 copy-start.1
  101.4 3.5 %copy.20 = f32[5,64,2048]{2,1,0:T(8,128)} copy(f32[5,64,2048]{2,1,0:T(8,128)} %get-tuple-element.4) | data formatting | bytes 5242880
  105.0 0.0 copy-done.1
  105.0 0.6 copy.21
  (1 shorter events, 0.0 us)
Async XLA Ops:
  0.6 5.7 %copy-start = (f32[6,5,5,2048]{3,0,2,1:T(8,128)S(1)}, f32[6,5,5,2048]{3,0,2,1:T(8,128)}, u32[]{:S(2)}) copy-start(f32[6,5,5,2048]{3,0,2,1:T(8,128)} %param.12) | copy-start | bytes 3686404
  101.4 3.6 %copy-start.1 = (f32[64,64]{1,0:T(8,128)S(1)}, f32[64,64]{1,0:T(8,128)}, u32[]{:S(2)}) copy-start(f32[64,64]{1,0:T(8,128)} %get-tuple-element.5) | copy-start | bytes 49156

commit v2 on v1

--- a/solution.py
+++ b/solution.py
@@ -10,9 +10,11 @@
 
 VARS = 5
 NBR = 6
+BY_MATMUL = 3
 COMPS = 3
 LANES = 128
 TILES = 8
+GANG = 4
 MESH = pl.DeviceIdType.MESH
 F32 = jnp.float32
 BF16 = jnp.bfloat16
@@ -29,15 +31,15 @@
 
 
 def kernel(
-    count, cap, modes, cells, scale,
-    payload_ref, dest_ref, nbr_ref, coupling_ref, inv_ref,
-    basis_ref, factor_ref,
-    outgoing, arrived, loads, tag_rows, hot, scaled, start, first, second, gathered,
+    count, cap, modes, cells,
+    shapes_ref, weights_ref, dest_ref, cell_ref, nbr_ref, coupling_ref, inv_ref,
+    state_ref, table_ref,
+    tail, outgoing, arrived, loads, tag_rows, hot, scaled, start, middle, first, second, gathered,
     edges, halos, part, sums, whole,
-    send_a, recv_a, send_h, recv_h, send_g, recv_g, send_w, recv_w,
+    send_a, recv_a, send_h, recv_h, send_g, recv_g, send_w, recv_w, state_sem,
 ):
     me = lax.axis_index("slab")
-    nodes = dest_ref.shape[0]
+    nodes = dest_ref.shape[1]
     groups = LANES // cap
     width = modes // groups
     rows = COMPS * width + 16
@@ -59,23 +61,25 @@
     halos[...] = jnp.zeros_like(halos)
 
     dest = dest_ref[...]
+    height = -(-count // 16) * 16
+    names = dest == lax.broadcasted_iota(jnp.int32, (height, nodes), 0)
+    earlier = (
+        lax.broadcasted_iota(jnp.int32, (nodes, nodes), 0)
+        < lax.broadcasted_iota(jnp.int32, (nodes, nodes), 1)
+    )
+    before = dot_f32(names.astype(F32).astype(BF16), earlier.astype(F32).astype(BF16))
+    rank = jnp.sum(jnp.where(names, before, 0.0), axis=0, keepdims=True)
+    place = jnp.broadcast_to(dest.astype(F32) * LANES + rank, (8, nodes)).T[:, 0:1].astype(jnp.int32)
     lane = lax.broadcasted_iota(jnp.int32, (nodes, LANES), 1)
-    names = dest == lane
-    earlier = (
-        lax.broadcasted_iota(jnp.int32, (nodes, nodes), 1)
-        < lax.broadcasted_iota(jnp.int32, (nodes, nodes), 0)
-    )
-    before = dot_f32(earlier.astype(F32).astype(BF16), names.astype(F32).astype(BF16))
-    rank = jnp.sum(jnp.where(names, before, 0.0), axis=1, keepdims=True).astype(jnp.int32)
-    place = dest * LANES + rank
-    turned = payload_ref[...].T
+    tail[0 : COMPS * VARS] = weights_ref[...]
+    tail[COMPS * VARS : COMPS * VARS + 1] = cell_ref[...].astype(F32)
     pieces = []
     for group in range(groups):
         taken = [
-            turned[comp * modes + group * width : comp * modes + (group + 1) * width]
+            shapes_ref[comp * modes + group * width : comp * modes + (group + 1) * width]
             for comp in range(COMPS)
         ]
-        pieces.append(jnp.concatenate(taken + [turned[COMPS * modes : COMPS * modes + 16]], axis=0))
+        pieces.append(jnp.concatenate(taken + [tail[...]], axis=0))
     packed = jnp.concatenate(split_two(jnp.concatenate(pieces, axis=1)), axis=0)
 
     def pack_for(slab):
@@ -102,7 +106,7 @@
 
     def hot_step(block, carry):
         at = pl.ds(pl.multiple_of(block * span, span), span)
-        for slot in range(NBR):
+        for slot in range(BY_MATMUL):
             names_now = nbr_ref[slot : slot + 1, at]
             local = jnp.where(names_now >= 0, names_now - (first_cell + block * span), -1)
             hot[block, :, slot * span : (slot + 1) * span] = (window == local).astype(F32).astype(BF16)
@@ -110,15 +114,16 @@
 
     lax.fori_loop(0, TILES, hot_step, 0)
 
-    def scale_step(slot, carry):
-        for out_var in range(VARS):
-            total = inv_ref[out_var, 0:1, :] * coupling_ref[slot, 0]
+    filled = nbr_ref[...] >= 0
+    for in_var in range(VARS):
+        def scale_step(out_var, carry):
+            total = inv_ref[out_var, 0:1, :] * coupling_ref[0, in_var]
             for mid in range(1, VARS):
-                total = total + inv_ref[out_var, mid : mid + 1, :] * coupling_ref[slot, mid]
-            scaled[slot, out_var] = total
-        return carry
-
-    lax.fori_loop(0, NBR, scale_step, 0)
+                total = total + inv_ref[out_var, mid : mid + 1, :] * coupling_ref[mid, in_var]
+            scaled[out_var, in_var] = jnp.where(filled, total, 0.0)
+            return carry
+
+        lax.fori_loop(0, VARS, scale_step, 0)
 
     def arrive_step(shift, carry):
         slab = lax.rem(me + shift, count)
@@ -173,26 +178,45 @@
             total = inv_ref[var, 0:1, at] * forcing[:modes]
             for mid in range(1, VARS):
                 total = total + inv_ref[var, mid : mid + 1, at] * forcing[mid * modes : (mid + 1) * modes]
-            start[block, var * modes : (var + 1) * modes] = total
+            start[block + 1, var * modes : (var + 1) * modes] = total
             keep(first, block, var, total)
             if side is not None:
                 edges[0, side, var * modes : (var + 1) * modes] = total
 
-    def sweep(source, target, block, side):
+    def sweep(source, wide, target, kept, block, side):
         at = pl.ds(pl.multiple_of(block * span, span), span)
         near = jnp.concatenate([source[block], source[block + 1], source[block + 2]], axis=1)
-        for slot in range(NBR):
+        for slot in range(BY_MATMUL):
             both = dot_f32(near, hot[block, :, slot * span : (slot + 1) * span])
             gathered[slot] = both[:tall] + both[tall:]
+        for half in range(span // LANES):
+            for slot in range(BY_MATMUL, NBR):
+                here = pl.ds(pl.multiple_of(block * span + half * LANES, LANES), LANES)
+                local = nbr_ref[slot : slot + 1, here] - (first_cell + block * span + half * LANES)
+                lanes = jnp.broadcast_to(jnp.bitwise_and(local, LANES - 1), (modes, LANES))
+                tile = jnp.broadcast_to(lax.shift_right_arithmetic(local, 7), (modes, LANES))
+                for var in range(VARS):
+                    picked = None
+                    for index in range(2 * span // LANES + 1):
+                        at_block, at_half = divmod(half + index, span // LANES)
+                        values = wide[
+                            block + at_block, var * modes : (var + 1) * modes,
+                            at_half * LANES : (at_half + 1) * LANES,
+                        ]
+                        taken = jnp.take_along_axis(values, lanes, axis=1, mode="promise_in_bounds")
+                        picked = taken if picked is None else jnp.where(tile == index, taken, picked)
+                    gathered[slot, var * modes : (var + 1) * modes, half * LANES : (half + 1) * LANES] = picked
         for var in range(VARS):
-            total = start[block, var * modes : (var + 1) * modes]
+            total = start[block + 1, var * modes : (var + 1) * modes]
             for slot in range(NBR):
                 for mid in range(VARS):
                     total = total - (
-                        scaled[slot, var, mid : mid + 1, at]
+                        scaled[var, mid, slot : slot + 1, at]
                         * gathered[slot, mid * modes : (mid + 1) * modes]
                     )
             keep(target, block, var, total)
+            if kept is not None:
+                kept[block + 1, var * modes : (var + 1) * modes] = total
             if side is not None:
                 edges[1, side, var * modes : (var + 1) * modes] = total
 
@@ -219,7 +243,7 @@
         def _():
             halo_copy(turn, 1).start()
 
-    def halo_take(turn, state):
+    def halo_take(turn, state, wide):
         @pl.when(me > 0)
         def _():
             halo_wait(turn, 0).wait()
@@ -230,7 +254,9 @@
 
         for side, block in ((0, -1), (1, TILES)):
             for var in range(VARS):
-                keep(state, block, var, halos[turn, side, var * modes : (var + 1) * modes])
+                value = halos[turn, side, var * modes : (var + 1) * modes]
+                keep(state, block, var, value)
+                wide[block + 1, var * modes : (var + 1) * modes] = value
 
     last = TILES - 1
     begin(0, 0)
@@ -244,23 +270,26 @@
     lax.fori_loop(1, last, begin_step, 0)
 
     def first_step(block, carry):
-        sweep(first, second, block, None)
+        sweep(first, start, second, middle, block, None)
         return carry
 
     def second_step(block, carry):
-        sweep(second, first, block, None)
+        sweep(second, middle, first, None, block, None)
         return carry
 
     lax.fori_loop(1, TILES // 2, first_step, 0)
-    halo_take(0, first)
-    sweep(first, second, 0, 0)
-    sweep(first, second, last, 1)
+    halo_take(0, first, start)
+    sweep(first, start, second, middle, 0, 0)
+    sweep(first, start, second, middle, last, 1)
     halo_send(1)
     lax.fori_loop(TILES // 2, last, first_step, 0)
     lax.fori_loop(1, last, second_step, 0)
-    halo_take(1, second)
-    sweep(second, first, 0, None)
-    sweep(second, first, last, None)
+    halo_take(1, second, middle)
+    sweep(second, middle, first, None, 0, None)
+    sweep(second, middle, first, None, last, None)
+
+    state_copy = pltpu.make_async_copy(first.at[pl.ds(1, TILES)], state_ref, state_sem)
+    state_copy.start()
 
     def gram_step(block, total):
         for var in range(VARS):
@@ -318,44 +347,65 @@
             remote(part.at[tile], sums.at[me], send_g.at[tile], recv_g.at[me], owner).wait_send()
             remote(whole.at[tile], whole.at[tile], send_w.at[0], recv_w.at[tile], owner).wait_recv()
 
-    row_at = lax.broadcasted_iota(jnp.int32, (modes, 2 * modes), 0)
-    col_at = lax.broadcasted_iota(jnp.int32, (modes, 2 * modes), 1)
-    table = jnp.concatenate([whole[tile] for tile in range(TILES)], axis=0)
-    table = jnp.where(col_at < modes, table, jnp.where(col_at - modes == row_at, 1.0, 0.0))
-    bands = [table[tile * high : (tile + 1) * high] for tile in range(TILES)]
-    inner = lax.broadcasted_iota(jnp.int32, (high, 1), 0)
-    for pivot_at in range(modes):
-        band, offset = pivot_at // high, pivot_at % high
-        row = bands[band][offset : offset + 1]
-        row = row * (1.0 / row[:, pivot_at : pivot_at + 1])
-        for tile in range(band, TILES):
-            column = bands[tile][:, pivot_at : pivot_at + 1]
-            if tile == band:
-                column = jnp.where(inner > offset, column, 0.0)
-            bands[tile] = bands[tile] - column * row
-    table = jnp.concatenate(bands, axis=0)
-    diagonal = jnp.sum(jnp.where(col_at == row_at, table, 0.0), axis=1, keepdims=True)
-    root = jnp.sqrt(diagonal)
-    factor_ref[...] = jnp.where(col_at >= row_at, table * (root / diagonal) * (1.0 / scale), 0.0)[:, :modes]
-    inverse = pltpu.roll(table * (scale / root), modes, 1)[:, :modes]
-    inv_high, inv_low = split_two(inverse)
-    mixer = jnp.concatenate([inv_high, inv_high, inv_low], axis=1)
-
-    def basis_step(block, carry):
-        at = pl.ds(pl.multiple_of(block * span, span), span)
-        for var in range(VARS):
-            top = first[block + 1, var * modes : (var + 1) * modes]
-            bottom = first[block + 1, tall + var * modes : tall + (var + 1) * modes]
-            basis_ref[var, :, at] = dot_f32(mixer, jnp.concatenate([top, bottom, top], axis=0))
-        return carry
-
-    lax.fori_loop(0, TILES, basis_step, 0)
+    table_ref[...] = jnp.concatenate([whole[tile] for tile in range(TILES)], axis=0)
+    state_copy.wait()
 
     @pl.when(lax.rem(me, step) == 0)
     def _():
         for shift in range(1, count):
             slab = lax.rem(me + shift, count)
             remote(whole.at[mine], whole.at[mine], send_w.at[slab], recv_w.at[mine], slab).wait_send()
+
+
+def finish(modes, scale, table_ref, state_ref, basis_ref, factor_ref, mixer):
+    high = modes // TILES
+    tall = VARS * modes
+
+    @pl.when(pl.program_id(0) == 0)
+    def _():
+        row_at = lax.broadcasted_iota(jnp.int32, (modes, 2 * modes), 0)
+        col_at = lax.broadcasted_iota(jnp.int32, (modes, 2 * modes), 1)
+        table = table_ref[...]
+        table = jnp.where(col_at < modes, table, jnp.where(col_at - modes == row_at, 1.0, 0.0))
+        bands = [table[tile * high : (tile + 1) * high] for tile in range(TILES)]
+        inner = lax.broadcasted_iota(jnp.int32, (high, 2 * modes), 0)
+        for pivot_at in range(0, modes, GANG):
+            band, offset = pivot_at // high, pivot_at % high
+            columns = [
+                {
+                    tile: jnp.broadcast_to(bands[tile][:, pivot_at + q : pivot_at + q + 1], (high, 2 * modes))
+                    for tile in range(band, TILES)
+                }
+                for q in range(GANG)
+            ]
+            rows = [bands[band][offset + q : offset + q + 1] for q in range(GANG)]
+            for q in range(GANG):
+                marks = [columns[q][band][offset + r : offset + r + 1] for r in range(GANG)]
+                inverse = 1.0 / marks[q]
+                row = rows[q] * inverse
+                for r in range(q + 1, GANG):
+                    ratio = marks[r] * inverse
+                    for tile in range(band, TILES):
+                        columns[r][tile] = columns[r][tile] - columns[q][tile] * ratio
+                    rows[r] = rows[r] - marks[r] * row
+                for tile in range(band, TILES):
+                    column = columns[q][tile]
+                    if tile == band:
+                        column = jnp.where(inner > offset + q, column, 0.0)
+                    bands[tile] = bands[tile] - column * row
+        table = jnp.concatenate(bands, axis=0)
+        diagonal = jnp.sum(jnp.where(col_at == row_at, table, 0.0), axis=1, keepdims=True)
+        root = jnp.sqrt(diagonal)
+        upper = jnp.where(col_at >= row_at, table * (root / diagonal) * (1.0 / scale), 0.0)
+        factor_ref[...] = upper[:, :modes]
+        inverse = pltpu.roll(table * (scale / root), modes, 1)[:, :modes]
+        inv_high, inv_low = split_two(inverse)
+        mixer[...] = jnp.concatenate([inv_high, inv_high, inv_low], axis=1)
+
+    for var in range(VARS):
+        top = state_ref[0, var * modes : (var + 1) * modes]
+        bottom = state_ref[0, tall + var * modes : tall + (var + 1) * modes]
+        basis_ref[var] = dot_f32(mixer[...], jnp.concatenate([top, bottom, top], axis=0))
 
 
 def local(
@@ -370,28 +420,27 @@
     rows = COMPS * (modes // groups) + 16
     tall = VARS * modes
     span = cells // TILES
-    payload = jnp.concatenate(
-        [mode_shapes, wall_coupling, owner_cell.astype(F32)[:, None], jnp.zeros((nodes, 48), F32)], axis=1
-    )
     scale = math.sqrt(VARS * cells * count)
     vmem = pl.BlockSpec(memory_space=pltpu.VMEM)
     dma = pltpu.SemaphoreType.DMA
-    return pl.pallas_call(
-        functools.partial(kernel, count, cap, modes, cells, scale),
+    state, table = pl.pallas_call(
+        functools.partial(kernel, count, cap, modes, cells),
         out_shape=(
-            jax.ShapeDtypeStruct((VARS, modes, cells), F32),
-            jax.ShapeDtypeStruct((modes, modes), F32),
+            jax.ShapeDtypeStruct((TILES, 2 * tall, span), BF16),
+            jax.ShapeDtypeStruct((modes, 2 * modes), F32),
         ),
-        in_specs=[vmem] * 5,
-        out_specs=(vmem, vmem),
+        in_specs=[vmem] * 7,
+        out_specs=(pl.BlockSpec(memory_space=pl.ANY), vmem),
         scratch_shapes=[
+            pltpu.VMEM((16, nodes), F32),
             pltpu.VMEM((count, rows, LANES), F32),
             pltpu.VMEM((count, rows, LANES), F32),
             pltpu.VMEM((2 * tall, count * cap), BF16),
             pltpu.VMEM((8, count * cap), F32),
-            pltpu.VMEM((TILES, 3 * span, NBR * span), BF16),
-            pltpu.VMEM((NBR, VARS, VARS, cells), F32),
-            pltpu.VMEM((TILES, tall, span), F32),
+            pltpu.VMEM((TILES, 3 * span, max(1, BY_MATMUL) * span), BF16),
+            pltpu.VMEM((VARS, VARS, NBR, cells), F32),
+            pltpu.VMEM((TILES + 2, tall, span), F32),
+            pltpu.VMEM((TILES + 2, tall, span), F32),
             pltpu.VMEM((TILES + 2, 2 * tall, span), BF16),
             pltpu.VMEM((TILES + 2, 2 * tall, span), BF16),
             pltpu.VMEM((NBR, tall, span), F32),
@@ -401,12 +450,32 @@
             pltpu.VMEM((count, modes // TILES, 2 * modes), F32),
             pltpu.VMEM((TILES, modes // TILES, 2 * modes), F32),
             dma((count,)), dma((count,)), dma((2, 2)), dma((2, 2)),
-            dma((TILES,)), dma((count,)), dma((count,)), dma((TILES,)),
+            dma((TILES,)), dma((count,)), dma((count,)), dma((TILES,)), dma,
         ],
         compiler_params=pltpu.CompilerParams(
             collective_id=0, has_side_effects=True, vmem_limit_bytes=58 * 1024 * 1024
         ),
-    )(payload, owner_dev, neighbours, coupling_blocks, inv_blocks)
+    )(
+        mode_shapes.T, wall_coupling.T, owner_dev.T, owner_cell.reshape(1, nodes), neighbours,
+        coupling_blocks.transpose(1, 2, 0, 3), inv_blocks,
+    )
+    return pl.pallas_call(
+        functools.partial(finish, modes, scale),
+        grid=(TILES,),
+        out_shape=(
+            jax.ShapeDtypeStruct((VARS, modes, cells), F32),
+            jax.ShapeDtypeStruct((modes, modes), F32),
+        ),
+        in_specs=[
+            pl.BlockSpec((modes, 2 * modes), lambda block: (0, 0)),
+            pl.BlockSpec((1, 2 * tall, span), lambda block: (block, 0, 0)),
+        ],
+        out_specs=(
+            pl.BlockSpec((VARS, modes, span), lambda block: (0, 0, block)),
+            pl.BlockSpec((modes, modes), lambda block: (0, 0)),
+        ),
+        scratch_shapes=[pltpu.VMEM((modes, 3 * modes), BF16)],
+    )(table, state)
 
 
 def solution(mesh):

time: 106 us -> 89.2 us (0.84)
  local copies, waits for them, and re-layouts: 10 us -> 0 us
  Pallas kernels: 93.1 us -> 88.3 us
  other arithmetic: 1.8 us -> 0 us
    unnamed x10 -> x0, local copies, waits for them, and re-layouts: 9.81 us -> none
    pallas_call x1 -> x2, Pallas kernels: 93.1 us -> 88.3 us  [the longest x1 79.5 us: local(): pl.pallas_call(functools.partial(kernel, count, cap, modes, cells), out_s...]
where the time goes in v2:
time: 89.2 us; the launch traced here: 89 us
  Pallas kernels  88.3 us (99%)
    pallas_call x1, Pallas kernels, local(): pl.pallas_call(functools.partial(kernel, count, cap, modes, cells), out_s...  79.5 us
    pallas_call x1, Pallas kernels, local(): pl.pallas_call(functools.partial(finish, modes, scale), grid=(TILES,), ou...  8.84 us

profile of v2, /device:TPU:0, one launch (start us, length us, event | category | flops | bytes accessed | tf_op | source)
XLA Modules:
  0.0 89.0 jit_solution(6317453963447439639)
XLA Ops:
  0.6 79.5 %shard_map.86 = (bf16[8,640,256]{2,1,0:T(8,128)(2,1)}, f32[64,128]{1,0:T(8,128)}) custom-call(f32[192,512]{1,0:T(8,128)} %bitcast.6, f32[15,512]{1,0:T(8,128)} %bitcast.7, s32[1,512]{1,0:T(1,128)} %bitcast.8, s32[1,512]{1,0:T(1,128)} %bitcast.9, s32[6,2048]{1,0:T(8,128)} %nbr_ref.1, f32[5,5,6,2048]{3,2,1,0:T(8,128)} %bitcast.5, f32[5,5,2048]{2,1,0:T(8,128)} %inv_ref.1), custom_call_target="tpu_custom_call" | custom-call | tf_op jit(solution)/shard_map/pallas_call | solution.py:426
  80.1 8.8 %shard_map.87 = (f32[5,64,2048]{2,1,0:T(8,128)}, f32[64,64]{1,0:T(8,128)}) custom-call(f32[64,128]{1,0:T(8,128)} %get-tuple-element.4.table_ref, bf16[8,640,256]{2,1,0:T(8,128)(2,1)} %get-tuple-element.5.state_ref), custom_call_target="tpu_custom_call" | custom-call | tf_op jit(solution)/shard_map/pallas_call | solution.py:462

commit v3 on v2

--- a/solution.py
+++ b/solution.py
@@ -14,7 +14,7 @@
 COMPS = 3
 LANES = 128
 TILES = 8
-GANG = 4
+GANG = 8
 MESH = pl.DeviceIdType.MESH
 F32 = jnp.float32
 BF16 = jnp.bfloat16
@@ -34,8 +34,8 @@
     count, cap, modes, cells,
     shapes_ref, weights_ref, dest_ref, cell_ref, nbr_ref, coupling_ref, inv_ref,
     state_ref, table_ref,
-    tail, outgoing, arrived, loads, tag_rows, hot, scaled, start, middle, first, second, gathered,
-    edges, halos, part, sums, whole,
+    tail, outgoing, arrived, loads, tag_rows, hot, scaled, start, middle, first, second, even, odd,
+    part, sums, whole,
     send_a, recv_a, send_h, recv_h, send_g, recv_g, send_w, recv_w, state_sem,
 ):
     me = lax.axis_index("slab")
@@ -58,7 +58,9 @@
         pl.semaphore_signal(
             barrier, inc=1, device_id={"slab": lax.rem(me + shift, count)}, device_id_type=MESH
         )
-    halos[...] = jnp.zeros_like(halos)
+    for wide in (start, middle):
+        wide[0] = jnp.zeros_like(wide[0])
+        wide[TILES + 1] = jnp.zeros_like(wide[0])
 
     dest = dest_ref[...]
     height = -(-count // 16) * 16
@@ -125,66 +127,130 @@
 
         lax.fori_loop(0, VARS, scale_step, 0)
 
-    def arrive_step(shift, carry):
-        slab = lax.rem(me + shift, count)
-        remote(outgoing.at[slab], arrived.at[slab], send_a.at[slab], recv_a.at[slab], slab).wait()
+    part_of = lax.broadcasted_iota(jnp.int32, (1, LANES), 1) // cap
+    depth = loads.shape[1]
+    per_chunk = depth // cap
+    chunks = count // per_chunk
+
+    def take_chunk(chunk):
+        for turn in range(per_chunk):
+            shift = chunk * per_chunk + turn
+            slab = lax.rem(me - shift + count, count)
+
+            @pl.when(shift > 0)
+            def _():
+                remote(outgoing.at[slab], arrived.at[slab], send_a.at[slab], recv_a.at[slab], slab).wait_recv()
+
+        for bunch in range(depth // LANES):
+            tags = jnp.zeros((1, LANES), F32)
+            built = [[None] * groups for _ in range(VARS)]
+            for turn in range(groups):
+                here = part_of == turn
+                shift = chunk * per_chunk + bunch * groups + turn
+                data = arrived[lax.rem(me - shift + count, count)]
+                base = COMPS * width
+                tags = jnp.where(here, data[base + 15 : base + 16], tags)
+                for var in range(VARS):
+                    load = data[base + COMPS * var : base + COMPS * var + 1] * data[:width]
+                    for comp in range(1, COMPS):
+                        at_row = base + COMPS * var + comp
+                        load = load + data[at_row : at_row + 1] * data[comp * width : (comp + 1) * width]
+                    for group in range(groups):
+                        turn_by = ((turn - group) * cap) % LANES
+                        moved = pltpu.roll(load, turn_by, 1) if turn_by else load
+                        kept = built[var][group]
+                        built[var][group] = moved if kept is None else jnp.where(here, moved, kept)
+            at = slice(bunch * LANES, (bunch + 1) * LANES)
+            for var in range(VARS):
+                high, low = split_two(jnp.concatenate(built[var], axis=0))
+                loads[var * modes : (var + 1) * modes, at] = high
+                loads[tall + var * modes : tall + (var + 1) * modes, at] = low
+            tag_rows[:, at] = jnp.broadcast_to(tags, (8, LANES))
+        return tag_rows[...].T[:, 0:1].astype(jnp.int32)
+
+    slot_cells = lax.broadcasted_iota(jnp.int32, (depth, span), 1)
+
+    def chunk_forcing(tag_column, block):
+        matches = (tag_column == slot_cells + block * span).astype(F32).astype(BF16)
+        both = dot_f32(loads[...], matches)
+        return both[:tall] + both[tall:]
+
+    tag_first = take_chunk(0)
+
+    def open_step(block, carry):
+        start[block + 1] = chunk_forcing(tag_first, block)
         return carry
 
-    lax.fori_loop(1, count, arrive_step, 0)
-
-    part_of = lax.broadcasted_iota(jnp.int32, (1, LANES), 1) // cap
-
-    def load_step(bunch, carry):
-        at = pl.ds(pl.multiple_of(bunch * LANES, LANES), LANES)
-        tags = jnp.zeros((1, LANES), F32)
-        built = [[None] * groups for _ in range(VARS)]
-        for turn in range(groups):
-            here = part_of == turn
-            data = arrived[bunch * groups + turn]
-            base = COMPS * width
-            tags = jnp.where(here, data[base + 15 : base + 16], tags)
-            for var in range(VARS):
-                load = data[base + COMPS * var : base + COMPS * var + 1] * data[:width]
-                for comp in range(1, COMPS):
-                    at_row = base + COMPS * var + comp
-                    load = load + data[at_row : at_row + 1] * data[comp * width : (comp + 1) * width]
-                for group in range(groups):
-                    turn_by = ((turn - group) * cap) % LANES
-                    moved = pltpu.roll(load, turn_by, 1) if turn_by else load
-                    kept = built[var][group]
-                    built[var][group] = moved if kept is None else jnp.where(here, moved, kept)
-        for var in range(VARS):
-            high, low = split_two(jnp.concatenate(built[var], axis=0))
-            loads[var * modes : (var + 1) * modes, at] = high
-            loads[tall + var * modes : tall + (var + 1) * modes, at] = low
-        tag_rows[:, at] = jnp.broadcast_to(tags, (8, LANES))
-        return carry
-
-    lax.fori_loop(0, count // groups, load_step, 0)
-    tag_column = tag_rows[...].T[:, 0:1].astype(jnp.int32)
-    slot_cells = lax.broadcasted_iota(jnp.int32, (count * cap, span), 1)
+    lax.fori_loop(0, TILES, open_step, 0)
+
+    def chunk_step(chunk, carry):
+        tag_column = take_chunk(chunk)
+
+        def add_step(block, carry):
+            start[block + 1] = start[block + 1] + chunk_forcing(tag_column, block)
+            return carry
+
+        return lax.fori_loop(0, TILES, add_step, carry)
+
+    lax.fori_loop(1, chunks - 1, chunk_step, 0)
+    tag_last = take_chunk(chunks - 1)
 
     def keep(state, block, var, value):
         high, low = split_two(value)
         state[block + 1, var * modes : (var + 1) * modes] = high
         state[block + 1, tall + var * modes : tall + (var + 1) * modes] = low
 
-    def begin(block, side):
+    def halo(wide, turn, side):
+        peer = me - 1 if side == 0 else me + 1
+        near, far = (1, TILES + 1) if side == 0 else (TILES, 0)
+        return remote(
+            wide.at[near], wide.at[far], send_h.at[turn, side], recv_h.at[turn, 1 - side], peer
+        )
+
+    def halo_arrival(wide, turn, side):
+        peer = me - 1 if side == 0 else me + 1
+        near, far = (1, 0) if side == 0 else (TILES, TILES + 1)
+        return remote(wide.at[near], wide.at[far], send_h.at[turn, side], recv_h.at[turn, side], peer)
+
+    def halo_send(wide, turn):
+        @pl.when(me > 0)
+        def _():
+            halo(wide, turn, 0).start()
+
+        @pl.when(me < count - 1)
+        def _():
+            halo(wide, turn, 1).start()
+
+    def halo_take(wide, turn, state):
+        @pl.when(me > 0)
+        def _():
+            halo_arrival(wide, turn, 0).wait()
+
+        @pl.when(me < count - 1)
+        def _():
+            halo_arrival(wide, turn, 1).wait()
+
+        for block in (-1, TILES):
+            for var in range(VARS):
+                keep(state, block, var, wide[block + 1, var * modes : (var + 1) * modes])
+
+    def begin_step(turn, carry):
+        block = lax.rem(turn * (TILES - 1), TILES)
         at = pl.ds(pl.multiple_of(block * span, span), span)
-        matches = (tag_column == slot_cells + block * span).astype(F32).astype(BF16)
-        both = dot_f32(loads[...], matches)
-        forcing = both[:tall] + both[tall:]
+        forcing = start[block + 1] + chunk_forcing(tag_last, block)
         for var in range(VARS):
             total = inv_ref[var, 0:1, at] * forcing[:modes]
             for mid in range(1, VARS):
                 total = total + inv_ref[var, mid : mid + 1, at] * forcing[mid * modes : (mid + 1) * modes]
             start[block + 1, var * modes : (var + 1) * modes] = total
             keep(first, block, var, total)
-            if side is not None:
-                edges[0, side, var * modes : (var + 1) * modes] = total
-
-    def sweep(source, wide, target, kept, block, side):
-        at = pl.ds(pl.multiple_of(block * span, span), span)
+        return carry
+
+    lax.fori_loop(0, 2, begin_step, 0)
+    halo_send(start, 0)
+    lax.fori_loop(2, TILES, begin_step, 0)
+
+    def gather(source, wide, gathered, block):
         near = jnp.concatenate([source[block], source[block + 1], source[block + 2]], axis=1)
         for slot in range(BY_MATMUL):
             both = dot_f32(near, hot[block, :, slot * span : (slot + 1) * span])
@@ -206,6 +272,9 @@
                         taken = jnp.take_along_axis(values, lanes, axis=1, mode="promise_in_bounds")
                         picked = taken if picked is None else jnp.where(tile == index, taken, picked)
                     gathered[slot, var * modes : (var + 1) * modes, half * LANES : (half + 1) * LANES] = picked
+
+    def mix(gathered, target, kept, block):
+        at = pl.ds(pl.multiple_of(block * span, span), span)
         for var in range(VARS):
             total = start[block + 1, var * modes : (var + 1) * modes]
             for slot in range(NBR):
@@ -217,77 +286,33 @@
             keep(target, block, var, total)
             if kept is not None:
                 kept[block + 1, var * modes : (var + 1) * modes] = total
-            if side is not None:
-                edges[1, side, var * modes : (var + 1) * modes] = total
-
-    def halo_copy(turn, side):
-        peer = me - 1 if side == 0 else me + 1
-        return remote(
-            edges.at[turn, side], halos.at[turn, 1 - side],
-            send_h.at[turn, side], recv_h.at[turn, 1 - side], peer,
-        )
-
-    def halo_wait(turn, side):
-        peer = me - 1 if side == 0 else me + 1
-        return remote(
-            edges.at[turn, side], halos.at[turn, side],
-            send_h.at[turn, side], recv_h.at[turn, side], peer,
-        )
-
-    def halo_send(turn):
-        @pl.when(me > 0)
-        def _():
-            halo_copy(turn, 0).start()
-
-        @pl.when(me < count - 1)
-        def _():
-            halo_copy(turn, 1).start()
-
-    def halo_take(turn, state, wide):
-        @pl.when(me > 0)
-        def _():
-            halo_wait(turn, 0).wait()
-
-        @pl.when(me < count - 1)
-        def _():
-            halo_wait(turn, 1).wait()
-
-        for side, block in ((0, -1), (1, TILES)):
-            for var in range(VARS):
-                value = halos[turn, side, var * modes : (var + 1) * modes]
-                keep(state, block, var, value)
-                wide[block + 1, var * modes : (var + 1) * modes] = value
-
-    last = TILES - 1
-    begin(0, 0)
-    begin(last, 1)
-    halo_send(0)
-
-    def begin_step(block, carry):
-        begin(block, None)
-        return carry
-
-    lax.fori_loop(1, last, begin_step, 0)
-
-    def first_step(block, carry):
-        sweep(first, start, second, middle, block, None)
-        return carry
-
-    def second_step(block, carry):
-        sweep(second, middle, first, None, block, None)
-        return carry
-
-    lax.fori_loop(1, TILES // 2, first_step, 0)
-    halo_take(0, first, start)
-    sweep(first, start, second, middle, 0, 0)
-    sweep(first, start, second, middle, last, 1)
-    halo_send(1)
-    lax.fori_loop(TILES // 2, last, first_step, 0)
-    lax.fori_loop(1, last, second_step, 0)
-    halo_take(1, second, middle)
-    sweep(second, middle, first, None, 0, None)
-    sweep(second, middle, first, None, last, None)
-
+
+    def sweep(source, wide, target, kept, turn):
+        def block_of(item):
+            return lax.rem(item + 1, TILES)
+
+        gather(source, wide, even, block_of(0))
+
+        def pair_step(pair, carry):
+            @pl.when(pair == TILES // 2 - 2)
+            def _():
+                halo_take(wide, turn, source)
+
+            item = 2 * pair
+            gather(source, wide, odd, block_of(item + 1))
+            mix(even, target, kept, block_of(item))
+            gather(source, wide, even, block_of(item + 2))
+            mix(odd, target, kept, block_of(item + 1))
+            return carry
+
+        lax.fori_loop(0, TILES // 2 - 1, pair_step, 0)
+        gather(source, wide, odd, 0)
+        mix(even, target, kept, TILES - 1)
+        mix(odd, target, kept, 0)
+
+    sweep(first, start, second, middle, 0)
+    halo_send(middle, 1)
+    sweep(second, middle, first, None, 1)
     state_copy = pltpu.make_async_copy(first.at[pl.ds(1, TILES)], state_ref, state_sem)
     state_copy.start()
 
@@ -347,6 +372,12 @@
             remote(part.at[tile], sums.at[me], send_g.at[tile], recv_g.at[me], owner).wait_send()
             remote(whole.at[tile], whole.at[tile], send_w.at[0], recv_w.at[tile], owner).wait_recv()
 
+    def sent_step(shift, carry):
+        slab = lax.rem(me + shift, count)
+        remote(outgoing.at[slab], arrived.at[me], send_a.at[slab], recv_a.at[me], slab).wait_send()
+        return carry
+
+    lax.fori_loop(1, count, sent_step, 0)
     table_ref[...] = jnp.concatenate([whole[tile] for tile in range(TILES)], axis=0)
     state_copy.wait()
 
@@ -435,8 +466,8 @@
             pltpu.VMEM((16, nodes), F32),
             pltpu.VMEM((count, rows, LANES), F32),
             pltpu.VMEM((count, rows, LANES), F32),
-            pltpu.VMEM((2 * tall, count * cap), BF16),
-            pltpu.VMEM((8, count * cap), F32),
+            pltpu.VMEM((2 * tall, 2 * LANES), BF16),
+            pltpu.VMEM((8, 2 * LANES), F32),
             pltpu.VMEM((TILES, 3 * span, max(1, BY_MATMUL) * span), BF16),
             pltpu.VMEM((VARS, VARS, NBR, cells), F32),
             pltpu.VMEM((TILES + 2, tall, span), F32),
@@ -444,8 +475,7 @@
             pltpu.VMEM((TILES + 2, 2 * tall, span), BF16),
             pltpu.VMEM((TILES + 2, 2 * tall, span), BF16),
             pltpu.VMEM((NBR, tall, span), F32),
-            pltpu.VMEM((2, 2, tall, span), F32),
-            pltpu.VMEM((2, 2, tall, span), F32),
+            pltpu.VMEM((NBR, tall, span), F32),
             pltpu.VMEM((TILES, modes // TILES, 2 * modes), F32),
             pltpu.VMEM((count, modes // TILES, 2 * modes), F32),
             pltpu.VMEM((TILES, modes // TILES, 2 * modes), F32),

time: 89.2 us -> 87.6 us (0.982)
  Pallas kernels: 88.3 us -> 86.7 us
    pallas_call x1, Pallas kernels: 79.5 us -> 78.4 us  [local(): pl.pallas_call(functools.partial(kernel, count, cap, modes, cells), out_s...]
where the time goes in v3:
time: 87.6 us; the launch traced here: 87.4 us
  Pallas kernels  86.7 us (99%)
    pallas_call x1, Pallas kernels, local(): pl.pallas_call(functools.partial(kernel, count, cap, modes, cells), out_s...  78.4 us
    pallas_call x1, Pallas kernels, local(): pl.pallas_call(functools.partial(finish, modes, scale), grid=(TILES,), ou...  8.28 us

profile of v3, /device:TPU:0, one launch (start us, length us, event | category | flops | bytes accessed | tf_op | source)
XLA Modules:
  0.0 87.4 jit_solution(4356659989185828989)
XLA Ops:
  0.6 78.4 %shard_map.86 = (bf16[8,640,256]{2,1,0:T(8,128)(2,1)}, f32[64,128]{1,0:T(8,128)}) custom-call(f32[192,512]{1,0:T(8,128)} %bitcast.6, f32[15,512]{1,0:T(8,128)} %bitcast.7, s32[1,512]{1,0:T(1,128)} %bitcast.8, s32[1,512]{1,0:T(1,128)} %bitcast.9, s32[6,2048]{1,0:T(8,128)} %nbr_ref.1, f32[5,5,6,2048]{3,2,1,0:T(8,128)} %bitcast.5, f32[5,5,2048]{2,1,0:T(8,128)} %inv_ref.1), custom_call_target="tpu_custom_call" | custom-call | tf_op jit(solution)/shard_map/pallas_call | solution.py:457
  79.1 8.3 %shard_map.87 = (f32[5,64,2048]{2,1,0:T(8,128)}, f32[64,64]{1,0:T(8,128)}) custom-call(f32[64,128]{1,0:T(8,128)} %get-tuple-element.4.table_ref, bf16[8,640,256]{2,1,0:T(8,128)(2,1)} %get-tuple-element.5.state_ref), custom_call_target="tpu_custom_call" | custom-call | tf_op jit(solution)/shard_map/pallas_call | solution.py:492

commit v4 on v3

--- a/solution.py
+++ b/solution.py
@@ -10,10 +10,10 @@
 
 VARS = 5
 NBR = 6
-BY_MATMUL = 3
 COMPS = 3
 LANES = 128
 TILES = 8
+BAND = 32
 GANG = 8
 MESH = pl.DeviceIdType.MESH
 F32 = jnp.float32
@@ -34,7 +34,7 @@
     count, cap, modes, cells,
     shapes_ref, weights_ref, dest_ref, cell_ref, nbr_ref, coupling_ref, inv_ref,
     state_ref, table_ref,
-    tail, outgoing, arrived, loads, tag_rows, hot, scaled, start, middle, first, second, even, odd,
+    tail, outgoing, arrived, loads, tag_rows, scaled, start, middle, final,
     part, sums, whole,
     send_a, recv_a, send_h, recv_h, send_g, recv_g, send_w, recv_w, state_sem,
 ):
@@ -102,19 +102,6 @@
 
     lax.fori_loop(1, count, send_step, 0)
     arrived[me] = pack_for(me)
-
-    first_cell = me * cells - span
-    window = lax.broadcasted_iota(jnp.int32, (3 * span, span), 0)
-
-    def hot_step(block, carry):
-        at = pl.ds(pl.multiple_of(block * span, span), span)
-        for slot in range(BY_MATMUL):
-            names_now = nbr_ref[slot : slot + 1, at]
-            local = jnp.where(names_now >= 0, names_now - (first_cell + block * span), -1)
-            hot[block, :, slot * span : (slot + 1) * span] = (window == local).astype(F32).astype(BF16)
-        return carry
-
-    lax.fori_loop(0, TILES, hot_step, 0)
 
     filled = nbr_ref[...] >= 0
     for in_var in range(VARS):
@@ -195,11 +182,6 @@
     lax.fori_loop(1, chunks - 1, chunk_step, 0)
     tag_last = take_chunk(chunks - 1)
 
-    def keep(state, block, var, value):
-        high, low = split_two(value)
-        state[block + 1, var * modes : (var + 1) * modes] = high
-        state[block + 1, tall + var * modes : tall + (var + 1) * modes] = low
-
     def halo(wide, turn, side):
         peer = me - 1 if side == 0 else me + 1
         near, far = (1, TILES + 1) if side == 0 else (TILES, 0)
@@ -221,7 +203,7 @@
         def _():
             halo(wide, turn, 1).start()
 
-    def halo_take(wide, turn, state):
+    def halo_take(wide, turn):
         @pl.when(me > 0)
         def _():
             halo_arrival(wide, turn, 0).wait()
@@ -230,9 +212,6 @@
         def _():
             halo_arrival(wide, turn, 1).wait()
 
-        for block in (-1, TILES):
-            for var in range(VARS):
-                keep(state, block, var, wide[block + 1, var * modes : (var + 1) * modes])
 
     def begin_step(turn, carry):
         block = lax.rem(turn * (TILES - 1), TILES)
@@ -243,85 +222,75 @@
             for mid in range(1, VARS):
                 total = total + inv_ref[var, mid : mid + 1, at] * forcing[mid * modes : (mid + 1) * modes]
             start[block + 1, var * modes : (var + 1) * modes] = total
-            keep(first, block, var, total)
         return carry
 
     lax.fori_loop(0, 2, begin_step, 0)
     halo_send(start, 0)
     lax.fori_loop(2, TILES, begin_step, 0)
 
-    def gather(source, wide, gathered, block):
-        near = jnp.concatenate([source[block], source[block + 1], source[block + 2]], axis=1)
-        for slot in range(BY_MATMUL):
-            both = dot_f32(near, hot[block, :, slot * span : (slot + 1) * span])
-            gathered[slot] = both[:tall] + both[tall:]
-        for half in range(span // LANES):
-            for slot in range(BY_MATMUL, NBR):
+    first_cell = me * cells - span
+
+    def sweep(wide, turn, put):
+        def block_step(item, carry):
+            @pl.when(item == TILES - 2)
+            def _():
+                halo_take(wide, turn)
+
+            block = lax.rem(item + 1, TILES)
+            for half in range(span // LANES):
                 here = pl.ds(pl.multiple_of(block * span + half * LANES, LANES), LANES)
-                local = nbr_ref[slot : slot + 1, here] - (first_cell + block * span + half * LANES)
-                lanes = jnp.broadcast_to(jnp.bitwise_and(local, LANES - 1), (modes, LANES))
-                tile = jnp.broadcast_to(lax.shift_right_arithmetic(local, 7), (modes, LANES))
-                for var in range(VARS):
-                    picked = None
-                    for index in range(2 * span // LANES + 1):
-                        at_block, at_half = divmod(half + index, span // LANES)
-                        values = wide[
-                            block + at_block, var * modes : (var + 1) * modes,
-                            at_half * LANES : (at_half + 1) * LANES,
-                        ]
-                        taken = jnp.take_along_axis(values, lanes, axis=1, mode="promise_in_bounds")
-                        picked = taken if picked is None else jnp.where(tile == index, taken, picked)
-                    gathered[slot, var * modes : (var + 1) * modes, half * LANES : (half + 1) * LANES] = picked
-
-    def mix(gathered, target, kept, block):
-        at = pl.ds(pl.multiple_of(block * span, span), span)
-        for var in range(VARS):
-            total = start[block + 1, var * modes : (var + 1) * modes]
-            for slot in range(NBR):
-                for mid in range(VARS):
-                    total = total - (
-                        scaled[var, mid, slot : slot + 1, at]
-                        * gathered[slot, mid * modes : (mid + 1) * modes]
-                    )
-            keep(target, block, var, total)
-            if kept is not None:
-                kept[block + 1, var * modes : (var + 1) * modes] = total
-
-    def sweep(source, wide, target, kept, turn):
-        def block_of(item):
-            return lax.rem(item + 1, TILES)
-
-        gather(source, wide, even, block_of(0))
-
-        def pair_step(pair, carry):
-            @pl.when(pair == TILES // 2 - 2)
-            def _():
-                halo_take(wide, turn, source)
-
-            item = 2 * pair
-            gather(source, wide, odd, block_of(item + 1))
-            mix(even, target, kept, block_of(item))
-            gather(source, wide, even, block_of(item + 2))
-            mix(odd, target, kept, block_of(item + 1))
+                across = slice(half * LANES, (half + 1) * LANES)
+                lanes, tile = [], []
+                for slot in range(NBR):
+                    local = nbr_ref[slot : slot + 1, here] - (first_cell + block * span + half * LANES)
+                    lanes.append(jnp.broadcast_to(jnp.bitwise_and(local, LANES - 1), (BAND, LANES)))
+                    tile.append(jnp.broadcast_to(lax.shift_right_arithmetic(local, 7), (BAND, LANES)))
+                for base in range(0, modes, BAND):
+                    totals = [
+                        start[block + 1, var * modes + base : var * modes + base + BAND, across]
+                        for var in range(VARS)
+                    ]
+                    for slot in range(NBR):
+                        for mid in range(VARS):
+                            down = slice(mid * modes + base, mid * modes + base + BAND)
+                            picked = None
+                            for index in range(2 * span // LANES + 1):
+                                at_block, at_half = divmod(half + index, span // LANES)
+                                values = wide[
+                                    block + at_block, down, at_half * LANES : (at_half + 1) * LANES
+                                ]
+                                taken = jnp.take_along_axis(
+                                    values, lanes[slot], axis=1, mode="promise_in_bounds"
+                                )
+                                picked = taken if picked is None else jnp.where(tile[slot] == index, taken, picked)
+                            for var in range(VARS):
+                                totals[var] = totals[var] - scaled[var, mid, slot : slot + 1, here] * picked
+                    for var in range(VARS):
+                        put(block, slice(var * modes + base, var * modes + base + BAND), across, totals[var])
             return carry
 
-        lax.fori_loop(0, TILES // 2 - 1, pair_step, 0)
-        gather(source, wide, odd, 0)
-        mix(even, target, kept, TILES - 1)
-        mix(odd, target, kept, 0)
-
-    sweep(first, start, second, middle, 0)
+        lax.fori_loop(0, TILES, block_step, 0)
+
+    def put_middle(block, down, across, value):
+        middle[block + 1, down, across] = value
+
+    def put_final(block, down, across, value):
+        high, low = split_two(value)
+        final[block, down, across] = high
+        final[block, slice(tall + down.start, tall + down.stop), across] = low
+
+    sweep(start, 0, put_middle)
     halo_send(middle, 1)
-    sweep(second, middle, first, None, 1)
-    state_copy = pltpu.make_async_copy(first.at[pl.ds(1, TILES)], state_ref, state_sem)
+    sweep(middle, 1, put_final)
+    state_copy = pltpu.make_async_copy(final, state_ref, state_sem)
     state_copy.start()
 
     def gram_step(block, total):
         for var in range(VARS):
             stack = jnp.concatenate(
                 [
-                    first[block + 1, var * modes : (var + 1) * modes],
-                    first[block + 1, tall + var * modes : tall + (var + 1) * modes],
+                    final[block, var * modes : (var + 1) * modes],
+                    final[block, tall + var * modes : tall + (var + 1) * modes],
                 ],
                 axis=0,
             )
@@ -468,14 +437,10 @@
             pltpu.VMEM((count, rows, LANES), F32),
             pltpu.VMEM((2 * tall, 2 * LANES), BF16),
             pltpu.VMEM((8, 2 * LANES), F32),
-            pltpu.VMEM((TILES, 3 * span, max(1, BY_MATMUL) * span), BF16),
             pltpu.VMEM((VARS, VARS, NBR, cells), F32),
             pltpu.VMEM((TILES + 2, tall, span), F32),
             pltpu.VMEM((TILES + 2, tall, span), F32),
-            pltpu.VMEM((TILES + 2, 2 * tall, span), BF16),
-            pltpu.VMEM((TILES + 2, 2 * tall, span), BF16),
-            pltpu.VMEM((NBR, tall, span), F32),
-            pltpu.VMEM((NBR, tall, span), F32),
+            pltpu.VMEM((TILES, 2 * tall, span), BF16),
             pltpu.VMEM((TILES, modes // TILES, 2 * modes), F32),
             pltpu.VMEM((count, modes // TILES, 2 * modes), F32),
             pltpu.VMEM((TILES, modes // TILES, 2 * modes), F32),

time: 87.6 us -> 107 us (1.22)
  Pallas kernels: 86.7 us -> 106 us
    pallas_call x1, Pallas kernels: 78.4 us -> 97.3 us  [local(): pl.pallas_call(functools.partial(kernel, count, cap, modes, cells), out_s...]
where the time goes in v4:
time: 107 us; the launch traced here: 106 us
  Pallas kernels  106 us (99%)
    pallas_call x1, Pallas kernels, local(): pl.pallas_call(functools.partial(kernel, count, cap, modes, cells), out_s...  97.3 us
    pallas_call x1, Pallas kernels, local(): pl.pallas_call(functools.partial(finish, modes, scale), grid=(TILES,), ou...  8.28 us

profile of v4, /device:TPU:0, one launch (start us, length us, event | category | flops | bytes accessed | tf_op | source)
XLA Modules:
  0.0 106.2 jit_solution(5219402341836458394)
XLA Ops:
  0.6 97.3 %shard_map.86 = (bf16[8,640,256]{2,1,0:T(8,128)(2,1)}, f32[64,128]{1,0:T(8,128)}) custom-call(f32[192,512]{1,0:T(8,128)} %bitcast.6, f32[15,512]{1,0:T(8,128)} %bitcast.7, s32[1,512]{1,0:T(1,128)} %bitcast.8, s32[1,512]{1,0:T(1,128)} %bitcast.9, s32[6,2048]{1,0:T(8,128)} %nbr_ref.1, f32[5,5,6,2048]{3,2,1,0:T(8,128)} %bitcast.5, f32[5,5,2048]{2,1,0:T(8,128)} %inv_ref.1), custom_call_target="tpu_custom_call" | custom-call | tf_op jit(solution)/shard_map/pallas_call | solution.py:426
  98.0 8.3 %shard_map.87 = (f32[5,64,2048]{2,1,0:T(8,128)}, f32[64,64]{1,0:T(8,128)}) custom-call(f32[64,128]{1,0:T(8,128)} %get-tuple-element.4.table_ref, bf16[8,640,256]{2,1,0:T(8,128)(2,1)} %get-tuple-element.5.state_ref), custom_call_target="tpu_custom_call" | custom-call | tf_op jit(solution)/shard_map/pallas_call | solution.py:457

commit v5 on v3

--- a/solution.py
+++ b/solution.py
@@ -10,10 +10,11 @@
 
 VARS = 5
 NBR = 6
-BY_MATMUL = 3
+BY_MATMUL = 4
 COMPS = 3
 LANES = 128
 TILES = 8
+BAND = 32
 GANG = 8
 MESH = pl.DeviceIdType.MESH
 F32 = jnp.float32
@@ -250,48 +251,58 @@
     halo_send(start, 0)
     lax.fori_loop(2, TILES, begin_step, 0)
 
-    def gather(source, wide, gathered, block):
+    def gather(source, gathered, block):
         near = jnp.concatenate([source[block], source[block + 1], source[block + 2]], axis=1)
         for slot in range(BY_MATMUL):
             both = dot_f32(near, hot[block, :, slot * span : (slot + 1) * span])
             gathered[slot] = both[:tall] + both[tall:]
+
+    def mix(gathered, wide, target, kept, block):
         for half in range(span // LANES):
+            here = pl.ds(pl.multiple_of(block * span + half * LANES, LANES), LANES)
+            across = slice(half * LANES, (half + 1) * LANES)
+            lanes, tile = {}, {}
             for slot in range(BY_MATMUL, NBR):
-                here = pl.ds(pl.multiple_of(block * span + half * LANES, LANES), LANES)
                 local = nbr_ref[slot : slot + 1, here] - (first_cell + block * span + half * LANES)
-                lanes = jnp.broadcast_to(jnp.bitwise_and(local, LANES - 1), (modes, LANES))
-                tile = jnp.broadcast_to(lax.shift_right_arithmetic(local, 7), (modes, LANES))
+                lanes[slot] = jnp.broadcast_to(jnp.bitwise_and(local, LANES - 1), (BAND, LANES))
+                tile[slot] = jnp.broadcast_to(lax.shift_right_arithmetic(local, 7), (BAND, LANES))
+            for base in range(0, modes, BAND):
+                totals = [
+                    start[block + 1, var * modes + base : var * modes + base + BAND, across]
+                    for var in range(VARS)
+                ]
+                for slot in range(NBR):
+                    for mid in range(VARS):
+                        down = slice(mid * modes + base, mid * modes + base + BAND)
+                        if slot < BY_MATMUL:
+                            picked = gathered[slot, down, across]
+                        else:
+                            picked = None
+                            for index in range(2 * span // LANES + 1):
+                                at_block, at_half = divmod(half + index, span // LANES)
+                                values = wide[
+                                    block + at_block, down, at_half * LANES : (at_half + 1) * LANES
+                                ]
+                                taken = jnp.take_along_axis(
+                                    values, lanes[slot], axis=1, mode="promise_in_bounds"
+                                )
+                                picked = taken if picked is None else jnp.where(tile[slot] == index, taken, picked)
+                        for var in range(VARS):
+                            totals[var] = totals[var] - scaled[var, mid, slot : slot + 1, here] * picked
                 for var in range(VARS):
-                    picked = None
-                    for index in range(2 * span // LANES + 1):
-                        at_block, at_half = divmod(half + index, span // LANES)
-                        values = wide[
-                            block + at_block, var * modes : (var + 1) * modes,
-                            at_half * LANES : (at_half + 1) * LANES,
-                        ]
-                        taken = jnp.take_along_axis(values, lanes, axis=1, mode="promise_in_bounds")
-                        picked = taken if picked is None else jnp.where(tile == index, taken, picked)
-                    gathered[slot, var * modes : (var + 1) * modes, half * LANES : (half + 1) * LANES] = picked
-
-    def mix(gathered, target, kept, block):
-        at = pl.ds(pl.multiple_of(block * span, span), span)
-        for var in range(VARS):
-            total = start[block + 1, var * modes : (var + 1) * modes]
-            for slot in range(NBR):
-                for mid in range(VARS):
-                    total = total - (
-                        scaled[var, mid, slot : slot + 1, at]
-                        * gathered[slot, mid * modes : (mid + 1) * modes]
-                    )
-            keep(target, block, var, total)
-            if kept is not None:
-                kept[block + 1, var * modes : (var + 1) * modes] = total
+                    rows_at = slice(var * modes + base, var * modes + base + BAND)
+                    low_at = slice(tall + var * modes + base, tall + var * modes + base + BAND)
+                    high, low = split_two(totals[var])
+                    target[block + 1, rows_at, across] = high
+                    target[block + 1, low_at, across] = low
+                    if kept is not None:
+                        kept[block + 1, rows_at, across] = totals[var]
 
     def sweep(source, wide, target, kept, turn):
         def block_of(item):
             return lax.rem(item + 1, TILES)
 
-        gather(source, wide, even, block_of(0))
+        gather(source, even, block_of(0))
 
         def pair_step(pair, carry):
             @pl.when(pair == TILES // 2 - 2)
@@ -299,16 +310,16 @@
                 halo_take(wide, turn, source)
 
             item = 2 * pair
-            gather(source, wide, odd, block_of(item + 1))
-            mix(even, target, kept, block_of(item))
-            gather(source, wide, even, block_of(item + 2))
-            mix(odd, target, kept, block_of(item + 1))
+            gather(source, odd, block_of(item + 1))
+            mix(even, wide, target, kept, block_of(item))
+            gather(source, even, block_of(item + 2))
+            mix(odd, wide, target, kept, block_of(item + 1))
             return carry
 
         lax.fori_loop(0, TILES // 2 - 1, pair_step, 0)
-        gather(source, wide, odd, 0)
-        mix(even, target, kept, TILES - 1)
-        mix(odd, target, kept, 0)
+        gather(source, odd, 0)
+        mix(even, wide, target, kept, TILES - 1)
+        mix(odd, wide, target, kept, 0)
 
     sweep(first, start, second, middle, 0)
     halo_send(middle, 1)
@@ -468,14 +479,14 @@
             pltpu.VMEM((count, rows, LANES), F32),
             pltpu.VMEM((2 * tall, 2 * LANES), BF16),
             pltpu.VMEM((8, 2 * LANES), F32),
-            pltpu.VMEM((TILES, 3 * span, max(1, BY_MATMUL) * span), BF16),
+            pltpu.VMEM((TILES, 3 * span, BY_MATMUL * span), BF16),
             pltpu.VMEM((VARS, VARS, NBR, cells), F32),
             pltpu.VMEM((TILES + 2, tall, span), F32),
             pltpu.VMEM((TILES + 2, tall, span), F32),
             pltpu.VMEM((TILES + 2, 2 * tall, span), BF16),
             pltpu.VMEM((TILES + 2, 2 * tall, span), BF16),
-            pltpu.VMEM((NBR, tall, span), F32),
-            pltpu.VMEM((NBR, tall, span), F32),
+            pltpu.VMEM((BY_MATMUL, tall, span), F32),
+            pltpu.VMEM((BY_MATMUL, tall, span), F32),
             pltpu.VMEM((TILES, modes // TILES, 2 * modes), F32),
             pltpu.VMEM((count, modes // TILES, 2 * modes), F32),
             pltpu.VMEM((TILES, modes // TILES, 2 * modes), F32),

time: 87.6 us -> 85.9 us (0.981)
  Pallas kernels: 86.7 us -> 85 us
    pallas_call x1, Pallas kernels: 78.4 us -> 76.7 us  [local(): pl.pallas_call(functools.partial(kernel, count, cap, modes, cells), out_s...]
where the time goes in v5:
time: 85.9 us; the launch traced here: 85.6 us
  Pallas kernels  85 us (99%)
    pallas_call x1, Pallas kernels, local(): pl.pallas_call(functools.partial(kernel, count, cap, modes, cells), out_s...  76.7 us
    pallas_call x1, Pallas kernels, local(): pl.pallas_call(functools.partial(finish, modes, scale), grid=(TILES,), ou...  8.28 us

profile of v5, /device:TPU:0, one launch (start us, length us, event | category | flops | bytes accessed | tf_op | source)
XLA Modules:
  0.0 85.6 jit_solution(2426133916474375568)
XLA Ops:
  0.6 76.7 %shard_map.86 = (bf16[8,640,256]{2,1,0:T(8,128)(2,1)}, f32[64,128]{1,0:T(8,128)}) custom-call(f32[192,512]{1,0:T(8,128)} %bitcast.6, f32[15,512]{1,0:T(8,128)} %bitcast.7, s32[1,512]{1,0:T(1,128)} %bitcast.8, s32[1,512]{1,0:T(1,128)} %bitcast.9, s32[6,2048]{1,0:T(8,128)} %nbr_ref.1, f32[5,5,6,2048]{3,2,1,0:T(8,128)} %bitcast.5, f32[5,5,2048]{2,1,0:T(8,128)} %inv_ref.1), custom_call_target="tpu_custom_call" | custom-call | tf_op jit(solution)/shard_map/pallas_call | solution.py:468
  77.3 8.3 %shard_map.87 = (f32[5,64,2048]{2,1,0:T(8,128)}, f32[64,64]{1,0:T(8,128)}) custom-call(f32[64,128]{1,0:T(8,128)} %get-tuple-element.4.table_ref, bf16[8,640,256]{2,1,0:T(8,128)(2,1)} %get-tuple-element.5.state_ref), custom_call_target="tpu_custom_call" | custom-call | tf_op jit(solution)/shard_map/pallas_call | solution.py:503
